TPU v7x, 32 devices: a whole 2x2x4 slice. The times are simulated.
32 devices in a mesh: dp: 8 (over z, y), pair: 4 (over x, core).
Axes of the slice: x: 2, y: 2, z: 4, core: 2. Of those that a mesh axis runs over, the one named last changes fastest.
Arguments:
- actions: bfloat16 [4, 1536, 16, 256], P(None, ('dp', 'pair')), may hold values from -6 to 6
- observations: bfloat16 [4, 384, 1024], P(None, 'dp', 'pair'), may hold values from -6 to 6
- tsteps: int32 [4, 1536], P(None, ('dp', 'pair')), may hold values from 0 to 99
- lengths: int32 [4, 1536], P(None, ('dp', 'pair')), may hold values from 4 to 16
- cot_skip: bfloat16 [4, 1536, 16, 512], P(None, ('dp', 'pair')), may hold values from -6 to 6
- cot_down: bfloat16 [4, 1536, 8, 512], P(None, ('dp', 'pair')), may hold values from -6 to 6
- owners: int32 [62], replicated, may hold values from 0 to 7, as said below
- master: float32 [128, 128, 512], P('dp'), may hold values from -0.1875 to 0.1875
- moment_one: float32 [128, 128, 512], P('dp'), may hold values from -224 to 224
- moment_two: float32 [128, 128, 512], P('dp'), may hold values from 98.304 to 393.216
- small_master: float32 [10, 512], replicated, as said below
- small_one: float32 [10, 512], replicated, may hold values from -224 to 224
- small_two: float32 [10, 512], replicated, may hold values from 98.304 to 393.216
Outputs:
- skip_out: bfloat16 [4, 1536, 16, 512], P(None, ('dp', 'pair'))
- down_out: bfloat16 [4, 1536, 8, 512], P(None, ('dp', 'pair'))
- actions_grad: float32 [4, 1536, 16, 256], P(None, ('dp', 'pair'))
- observations_grad: float32 [4, 384, 1024], P(None, 'dp', 'pair')
- new_moment_one: float32 [128, 128, 512], P('dp')
- new_moment_two: float32 [128, 128, 512], P('dp')
- new_master: float32 [128, 128, 512], P('dp')
- new_small_one: float32 [10, 512], replicated
- new_small_two: float32 [10, 512], replicated
- new_small: float32 [10, 512], replicated
Inputs may be any that keep to these rules, and one draw needn't show every extreme that they name: `owners`: no index owns more than 16 blocks, and one owns exactly 16. `lengths`: frames at or past a window's length are padding. `small_master`: rows 1 and 6 are gains, the others biases.
All inputs are finite; a program needn't handle non-finite values.
Results may differ from a plain program's by a relative error of at most 0.0086.
Values may be sent and summed in bfloat16 or wider, within the bound.
No kernel may reach another device: no remote copies, remote signals or barrier semaphores. Data moves between devices by JAX's collectives and lax.ppermute only.
A program may use at most 192 MiB of HBM per device.

v0:
```python
import math

import jax
import jax.numpy as jnp
from jax import lax
from jax.sharding import PartitionSpec as P

CI = 256
C = 512
TE = 128
GROUPS = 8
KW = 5
H = 16
KD = 3
NSMALL = 10
STEP = 10
BLK = 128
COND = 1152
ROWS = 7936


BETA_ONE = 0.9
BETA_TWO = 0.999
EPS_ADAM = 1e-08
DECAY = 0.01
RATE_MATRIX = 0.1
RATE_SMALL = 1.0


def mish(value):
    return value * jnp.tanh(jax.nn.softplus(value))


def time_embed(step_ids, width):
    half = width // 2
    freq = jnp.exp(-math.log(10000.0) * jnp.arange(half, dtype=jnp.float32) / (half - 1))
    angle = step_ids.astype(jnp.float32)[:, None] * freq[None, :]
    return jnp.concatenate([jnp.sin(angle), jnp.cos(angle)], axis=1)


def group_norm(value, frame_mask, gain, bias):
    count_s, frames, chans = value.shape
    grouped = value.reshape(count_s, frames, GROUPS, chans // GROUPS)
    weight = frame_mask[:, :, None, None]
    count = jnp.sum(frame_mask, axis=1)[:, None] * (chans // GROUPS)
    mean = jnp.sum(grouped * weight, axis=(1, 3)) / count
    centered = grouped - mean[:, None, :, None]
    var = jnp.sum(centered * centered * weight, axis=(1, 3)) / count
    normed = centered * lax.rsqrt(var + 1e-05)[:, None, :, None]
    return normed.reshape(count_s, frames, chans) * gain + bias


def unfold(value, taps, stride):
    pad_width = (taps - 1) // 2
    padded = jnp.pad(value, ((0, 0), (pad_width, pad_width), (0, 0)))
    count = value.shape[1] // stride
    pieces = [
        padded[:, tap_index : tap_index + stride * (count - 1) + 1 : stride]
        for tap_index in range(taps)
    ]
    return jnp.concatenate(pieces, axis=2)


def fold_taps(grad_cols, taps, stride, length, channels):
    pad_width = (taps - 1) // 2
    count = grad_cols.shape[1]
    total = jnp.zeros((grad_cols.shape[0], length + 2 * pad_width, channels), jnp.float32)
    for tap_index in range(taps):
        total = total.at[:, tap_index : tap_index + stride * (count - 1) + 1 : stride].add(
            grad_cols[:, :, tap_index * channels : (tap_index + 1) * channels]
        )
    return total[:, pad_width : pad_width + length]


def slot_of(owners, slot_count):
    same = owners[:, None] == owners[None, :]
    order = jnp.arange(owners.shape[0], dtype=jnp.int32)
    earlier = order[:, None] > order[None, :]
    rank = jnp.sum((same & earlier).astype(jnp.int32), axis=1)
    return owners * slot_count + rank


def adamw(weight, first_m, second_m, grad, rate):
    first_new = BETA_ONE * first_m + (1.0 - BETA_ONE) * grad
    second_new = BETA_TWO * second_m + (1.0 - BETA_TWO) * grad * grad
    fix_one = 1.0 - BETA_ONE**STEP
    fix_two = 1.0 - BETA_TWO**STEP
    update = first_new / fix_one / (jnp.sqrt(second_new / fix_two) + EPS_ADAM) + DECAY * weight
    return (first_new, second_new, weight - rate * update)


def weight_grad(cols, grads):
    return jnp.einsum("nk,nc->kc", cols, grads, preferred_element_type=jnp.float32)


def body(
    actions,
    observations,
    tsteps,
    lengths,
    cot_skip,
    cot_down,
    owners,
    master,
    moment_one,
    moment_two,
    small_master,
    small_one,
    small_two,
):
    slot_count = master.shape[0]
    dp_count = lax.axis_size("dp")
    slots_all = dp_count * slot_count
    slot_index = slot_of(owners, slot_count)
    fresh = lax.all_gather(master.astype(jnp.bfloat16), "dp", axis=0, tiled=True)
    weights = fresh[slot_index].reshape(ROWS, C)
    offset = 0
    w_first = weights[offset : offset + KW * CI]
    offset = offset + KW * CI
    w_second = weights[offset : offset + KW * C]
    offset = offset + KW * C
    w_res = weights[offset : offset + CI]
    offset = offset + CI
    w_down = weights[offset : offset + KD * C]
    offset = offset + KD * C
    w_film = jnp.concatenate(
        [weights[offset : offset + COND], weights[offset + COND : offset + 2 * COND]], axis=1
    )
    b_film = jnp.concatenate([small_master[3], small_master[4]])
    shared = lax.all_gather(observations, "pair", axis=2, tiled=True)

    def micro_step(carry, item):
        x_block, obs_block, step_block, len_block, cot_one, cot_two = item
        sample_count = x_block.shape[0]
        frame_mask = (jnp.arange(H)[None, :] < len_block[:, None]).astype(jnp.float32)
        masked = x_block * frame_mask[:, :, None].astype(jnp.bfloat16)
        masked_flat = masked.reshape(-1, CI)
        condition = jnp.concatenate(
            [time_embed(step_block, TE), obs_block.astype(jnp.float32)], axis=1
        )
        cond_act, mish_back = jax.vjp(mish, condition)
        cond_low = cond_act.astype(jnp.bfloat16)
        modulation = jnp.dot(cond_low, w_film, preferred_element_type=jnp.float32) + b_film
        scale = modulation[:, :C]
        shift = modulation[:, C:]
        cols_first = unfold(masked, KW, 1).reshape(-1, KW * CI)
        first = (
            jnp.dot(cols_first, w_first, preferred_element_type=jnp.float32) + small_master[0]
        ).reshape(sample_count, H, C)

        def section_one(first_v, scale_v, shift_v, gain_v, bias_v):
            normed = mish(group_norm(first_v, frame_mask, gain_v, bias_v))
            return (scale_v[:, None, :] * normed + shift_v[:, None, :]) * frame_mask[:, :, None]

        hidden, back_one = jax.vjp(
            section_one, first, scale, shift, small_master[1], small_master[2]
        )
        hidden_low = hidden.astype(jnp.bfloat16)
        cols_second = unfold(hidden_low, KW, 1).reshape(-1, KW * C)
        second = (
            jnp.dot(cols_second, w_second, preferred_element_type=jnp.float32) + small_master[5]
        ).reshape(sample_count, H, C)
        branch = (
            jnp.dot(masked_flat, w_res, preferred_element_type=jnp.float32).reshape(
                sample_count, H, C
            )
            + small_master[8]
        )

        def section_two(second_v, gain_v, bias_v):
            return mish(group_norm(second_v, frame_mask, gain_v, bias_v))

        activated, back_two = jax.vjp(section_two, second, small_master[6], small_master[7])
        skip_low = (activated + branch).astype(jnp.bfloat16)
        cols_down = unfold(skip_low, KD, 2).reshape(-1, KD * C)
        reduced = (
            jnp.dot(cols_down, w_down, preferred_element_type=jnp.float32) + small_master[9]
        ).astype(jnp.bfloat16)
        reduced = reduced.reshape(sample_count, H // 2, C)
        cot_flat = cot_two.reshape(-1, C)
        g_down = weight_grad(cols_down, cot_flat)
        g_bias_down = jnp.sum(cot_flat.astype(jnp.float32), axis=0)
        d_cols_down = jnp.dot(cot_flat, w_down.T, preferred_element_type=jnp.float32).reshape(
            sample_count, H // 2, KD * C
        )
        d_skip = (cot_one.astype(jnp.float32) + fold_taps(d_cols_down, KD, 2, H, C)).astype(
            jnp.bfloat16
        )
        d_skip_flat = d_skip.reshape(-1, C)
        g_res = weight_grad(masked_flat, d_skip_flat)
        g_bias_res = jnp.sum(d_skip_flat.astype(jnp.float32), axis=0)
        d_masked_res = jnp.dot(d_skip_flat, w_res.T, preferred_element_type=jnp.float32).reshape(
            sample_count, H, CI
        )
        d_second, g_gain_two, g_bias_two = back_two(d_skip.astype(jnp.float32))
        d_second_low = d_second.astype(jnp.bfloat16).reshape(-1, C)
        g_second = weight_grad(cols_second, d_second_low)
        g_bias_second = jnp.sum(d_second_low.astype(jnp.float32), axis=0)
        d_cols_second = jnp.dot(
            d_second_low, w_second.T, preferred_element_type=jnp.float32
        ).reshape(sample_count, H, KW * C)
        d_hidden = fold_taps(d_cols_second, KW, 1, H, C)
        d_first, d_scale, d_shift, g_gain_one, g_bias_one = back_one(d_hidden)
        d_film_low = jnp.concatenate([d_scale, d_shift], axis=1).astype(jnp.bfloat16)
        g_film = weight_grad(cond_low, d_film_low)
        g_bias_film = jnp.sum(d_film_low.astype(jnp.float32), axis=0)
        d_condition = mish_back(jnp.dot(d_film_low, w_film.T, preferred_element_type=jnp.float32))[
            0
        ]
        d_obs = d_condition[:, TE:]
        d_first_low = d_first.astype(jnp.bfloat16).reshape(-1, C)
        g_first = weight_grad(cols_first, d_first_low)
        g_bias_first = jnp.sum(d_first_low.astype(jnp.float32), axis=0)
        d_cols_first = jnp.dot(d_first_low, w_first.T, preferred_element_type=jnp.float32).reshape(
            sample_count, H, KW * CI
        )
        d_masked = fold_taps(d_cols_first, KW, 1, H, CI) + d_masked_res
        d_input = d_masked * frame_mask[:, :, None]
        g_small = jnp.stack(
            [
                g_bias_first,
                g_gain_one,
                g_bias_one,
                g_bias_film[:C],
                g_bias_film[C:],
                g_bias_second,
                g_gain_two,
                g_bias_two,
                g_bias_res,
                g_bias_down,
            ]
        )
        carry = (
            carry[0] + g_first,
            carry[1] + g_second,
            carry[2] + g_res,
            carry[3] + g_down,
            carry[4] + g_film,
            carry[5] + g_small,
        )
        return (carry, (skip_low, reduced, d_input, d_obs))

    init = (
        jnp.zeros((KW * CI, C), jnp.float32),
        jnp.zeros((KW * C, C), jnp.float32),
        jnp.zeros((CI, C), jnp.float32),
        jnp.zeros((KD * C, C), jnp.float32),
        jnp.zeros((COND, 2 * C), jnp.float32),
        jnp.zeros((NSMALL, C), jnp.float32),
    )
    sums, stacked = lax.scan(
        micro_step, init, (actions, shared, tsteps, lengths, cot_skip, cot_down)
    )
    skip_out, down_out, actions_grad, obs_local = stacked
    observations_grad = lax.psum_scatter(obs_local, "pair", scatter_dimension=2, tiled=True)
    grad_rows = jnp.concatenate(
        [sums[0], sums[1], sums[2], sums[3], sums[4][:, :C], sums[4][:, C:]], axis=0
    )
    grad_small = lax.psum(sums[5], ("dp", "pair"))
    grad_rows = lax.psum(grad_rows.astype(jnp.bfloat16), "pair").astype(jnp.float32)
    owned = lax.psum_scatter(
        jnp.zeros((slots_all, BLK, C), jnp.float32)
        .at[slot_index]
        .set(grad_rows.reshape(-1, BLK, C)),
        "dp",
        scatter_dimension=0,
        tiled=True,
    )
    new_one, new_two, new_master = adamw(master, moment_one, moment_two, owned, RATE_MATRIX)
    small_first, small_second, new_small = adamw(
        small_master, small_one, small_two, grad_small, RATE_SMALL
    )
    return (
        skip_out,
        down_out,
        actions_grad,
        observations_grad,
        new_one,
        new_two,
        new_master,
        small_first,
        small_second,
        new_small,
    )


def solution(mesh):
    placed = (
        P(None, ("dp", "pair"), None, None),
        P(None, "dp", "pair"),
        P(None, ("dp", "pair")),
        P(None, ("dp", "pair")),
        P(None, ("dp", "pair"), None, None),
        P(None, ("dp", "pair"), None, None),
        P(),
        P("dp", None, None),
        P("dp", None, None),
        P("dp", None, None),
        P(),
        P(),
        P(),
    )
    return jax.shard_map(
        body,
        mesh=mesh,
        in_specs=placed,
        out_specs=(
            P(None, ("dp", "pair"), None, None),
            P(None, ("dp", "pair"), None, None),
            P(None, ("dp", "pair"), None, None),
            P(None, "dp", "pair"),
            P("dp", None, None),
            P("dp", None, None),
            P("dp", None, None),
            P(),
            P(),
            P(),
        ),
        check_vma=False,
    )
```

profile of v0, /device:TPU:0, one launch (start us, length us, event | category | flops | bytes accessed | tf_op | source)
XLA Modules:
  0.0 1941.8 jit_solution(10511889351235682839)
XLA Ops:
  12.4 8.4 all_gather.6
  20.8 220.7 %all-gather.2.cloned.1.call-done = bf16[128,128,512]{2,1,0:T(8,128)(2,1)} async-done(((bf16[16,128,512]{2,1,0:T(8,128)(2,1)}), bf16[128,128,512]{2,1,0:T(8,128)(2,1)}) %all-gather.2.cloned.1.call-update) | async-done | bytes 16777232 | tf_op jit(solution)/shard_map/all_gather | solution.py:115
  241.5 11.2 gather_fusion
  265.3 886.8 %while.42 = (s32[]{:T(128)}, f32[1280,512]{1,0:T(8,128)}, f32[2560,512]{1,0:T(8,128)}, f32[256,512]{1,0:T(8,128)}, f32[1536,512]{1,0:T(8,128)}, /*index=5*/f32[1...) while((s32[]{:T(128)}, f32[1280,512]{1,0:T(8,128)}, ...), condition=%wide.region_29.31_spmd.clone, body=%wide.region_1.30_spmd.clone.sunk | while | flops 11908618240 | bytes 458313376 | solution.py:251
  366.8 8.6 scatter-add.122
  379.2 8.6 scatter-add.123
  391.7 8.6 scatter-add.124
  404.1 8.6 scatter-add.125
  583.9 8.6 scatter-add.122
  596.3 8.6 scatter-add.123
  608.8 8.6 scatter-add.124
  621.2 8.6 scatter-add.125
  629.9 5.5 multiply_reduce_fusion.21
  655.9 5.5 fusion.192
  805.5 8.6 scatter-add.122
  817.9 8.6 scatter-add.123
  830.4 8.6 scatter-add.124
  842.8 8.6 scatter-add.125
  877.4 5.5 fusion.192
  1026.8 8.6 scatter-add.122
  1039.3 8.6 scatter-add.123
  1051.7 8.6 scatter-add.124
  1064.1 8.6 scatter-add.125
  1098.8 5.5 fusion.192
  1165.8 146.9 %all-reduce.7.cloned.1.call-done = bf16[62,128,512]{2,1,0:T(8,128)(2,1)} async-done(((bf16[62,128,512]{2,1,0:T(8,128)(2,1)}), bf16[62,128,512]{2,1,0:T(8,128)(2,1)}) %all-reduce.7.cloned.1.call-update) | async-done | bytes 8126480 | tf_op jit(solution)/shard_map/psum | solution.py:260
  1312.7 11.2 reshape.766
  1323.9 11.3 broadcast_in_dim.133
  1335.2 30.0 %scatter_fusion.3 = f32[128,128,512]{2,1,0:T(8,128)} fusion(f32[128,128,512]{2,1,0:T(8,128)} %broadcast_in_dim.133, s32[62]{0:T(128)S(1)} %copy-done.65, f32[62,128,512]{2,1,0:T(8,128)} %reshape.766), kind=kCustom, calls=%fused_computation.4 | custom fusion | bytes 48759032 | tf_op jit(solution)/shard_map/scatter | solution.py:264
  1366.0 42.3 %psum.15 = f32[10,512]{1,0:T(8,128)S(1)} all-reduce(f32[10,512]{1,0:T(8,128)S(1)} %copy-done.42), channel_id=1, replica_groups=mesh['dp'=8,'pair'=4] {'dp','pair'}, use_global_device_ids=true, to_apply=%region_34.36 | all-reduce | flops 5120 | bytes 40960 | tf_op jit(solution)/shard_map/psum | solution.py:259
  1408.9 500.8 %reduce-scatter.5.cloned.1.call-done = f32[16,128,512]{2,1,0:T(8,128)} async-done(((f32[128,128,512]{2,1,0:T(8,128)}), f32[16,128,512]{2,1,0:T(8,128)}) %reduce-scatter.5.cloned.1.call-update) | async-done | bytes 4194320 | tf_op jit(solution)/shard_map/reduce_scatter | solution.py:261
  1909.7 11.1 multiply_subtract_fusion
  1920.8 14.2 reduce-scatter.3.cloned.1.call-done
  (1020 shorter events, 749.2 us)
Async XLA Ops:
  7.2 234.3 %all-gather.2.cloned.1.call-start = ((), (), s32[]{:S(2)}) async-start(), calls=%async_computation.2 | async-start | bytes 18874368 | tf_op jit(solution)/shard_map/all_gather | solution.py:115
  11.1 1301.6 %all-reduce.7.cloned.1.call-start = ((), (), s32[]{:S(2)}) async-start(), calls=%async_computation.4 | async-start | bytes 16252928 | tf_op jit(solution)/shard_map/psum | solution.py:260
  265.5 8.5 copy-start.3
  265.5 8.5 copy-start.56
  267.7 20.1 %copy-start.11 = (f32[48,16]{1,0:T(8,128)}, f32[48,16]{1,0:T(8,128)S(1)}, u32[]{:S(2)}) copy-start(f32[48,16]{1,0:T(8,128)S(1)} %get-tuple-element.992) | copy-start | bytes 9220 | tf_op jit(solution)/shard_map/while
  274.7 13.1 copy-start.24
  436.3 7.2 slice-start
  483.0 8.5 copy-start.3
  483.1 8.5 copy-start.56
  485.2 20.1 %copy-start.11 = (f32[48,16]{1,0:T(8,128)}, f32[48,16]{1,0:T(8,128)S(1)}, u32[]{:S(2)}) copy-start(f32[48,16]{1,0:T(8,128)S(1)} %get-tuple-element.992) | copy-start | bytes 9220 | tf_op jit(solution)/shard_map/while
  492.2 13.1 copy-start.24
  653.5 7.9 slice-start
  676.8 6.7 copy-start.21
  676.8 6.7 copy-start.59
  704.4 8.5 copy-start.3
  704.4 8.5 copy-start.56
  706.5 20.1 %copy-start.11 = (f32[48,16]{1,0:T(8,128)}, f32[48,16]{1,0:T(8,128)S(1)}, u32[]{:S(2)}) copy-start(f32[48,16]{1,0:T(8,128)S(1)} %get-tuple-element.992) | copy-start | bytes 9220 | tf_op jit(solution)/shard_map/while
  713.6 13.1 copy-start.24
  875.0 7.9 slice-start
  898.2 6.7 copy-start.21
  926.0 8.5 copy-start.3
  926.0 8.5 copy-start.56
  928.1 20.1 %copy-start.11 = (f32[48,16]{1,0:T(8,128)}, f32[48,16]{1,0:T(8,128)S(1)}, u32[]{:S(2)}) copy-start(f32[48,16]{1,0:T(8,128)S(1)} %get-tuple-element.992) | copy-start | bytes 9220 | tf_op jit(solution)/shard_map/while
  935.2 13.1 copy-start.24
  1096.4 7.9 slice-start
  1119.7 6.7 copy-start.21
  1119.8 6.7 copy-start.59
  1165.7 744.0 %reduce-scatter.5.cloned.1.call-start = ((), (), s32[]{:S(2)}) async-start(), calls=%async_computation.5 | async-start | bytes 37748736 | tf_op jit(solution)/shard_map/reduce_scatter | solution.py:261
  1323.9 11.3 copy-start.65
  1365.2 43.0 %copy-start.62 = (f32[10,512]{1,0:T(8,128)S(1)}, f32[10,512]{1,0:T(8,128)}, u32[]{:S(2)}) copy-start(f32[10,512]{1,0:T(8,128)} %param.48) | copy-start | bytes 61444
  1365.2 43.0 %copy-start.63 = (f32[10,512]{1,0:T(8,128)S(1)}, f32[10,512]{1,0:T(8,128)}, u32[]{:S(2)}) copy-start(f32[10,512]{1,0:T(8,128)} %param.47) | copy-start | bytes 61444
  1365.2 569.8 %reduce-scatter.3.cloned.1.call-start = ((), (), s32[]{:S(2)}) async-start(), calls=%async_computation.3 | async-start | bytes 983040 | tf_op jit(solution)/shard_map/reduce_scatter | solution.py:255
  (215 other events, 689.7 us)
Sparse Core Ops, SparseCore 0:
  11.2 230.2 all-gather.1
  1165.8 146.7 all-reduce.6
  1365.4 544.3 reduce-scatter.4
  1912.7 22.2 reduce-scatter.2
where the time goes:
time: 1950 us; the launch traced here: 1940 us
  waiting for transfers between devices  883 us (45%)
  local copies, waits for them, and re-layouts  470 us (24%)
  other arithmetic  371 us (19%)
  matrix products  143 us (7%)
  blocking collectives  50.6 us (3%)
    reduce_scatter x1, waiting for transfers between devices, body(): lax.psum_scatter(jnp.zeros((slots_all, BLK, C), jnp.float32).at[slot_inde...  501 us
    all_gather x1, waiting for transfers between devices, body(): lax.all_gather(master.astype(jnp.bfloat16), 'dp', axis=0, tiled=True)  221 us
    scatter-add x40, local copies, waits for them, and re-layouts, fold_taps(): total.at[:, tap_index:tap_index + stride * (count - 1) + 1:stride]  174 us
    psum x1, waiting for transfers between devices, body(): lax.psum(grad_rows.astype(jnp.bfloat16), 'pair').astype(jnp.float32)  147 us
    dot_general x20, matrix products, weight_grad(): jnp.einsum('nk,nc->kc', cols, grads, preferred_element_type=jnp.float32)  73.5 us
    add x40, other arithmetic, fold_taps(): total.at[:, tap_index:tap_index + stride * (count - 1) + 1:stride]  72.5 us
    while x488, local copies, waits for them, and re-layouts  43.5 us
    scatter-add x12, other arithmetic, fold_taps(): total.at[:, tap_index:tap_index + stride * (count - 1) + 1:stride]  42.5 us
  transfers between devices with their start and end apart: 4, of which 4 were waited for; matrix products, arithmetic and copies ran while one was open for 1% of the time, Pallas kernels for 0%

commit v1 on v0

v1 whole, which is shorter than its diff:
```python
import functools
import math

import jax
import jax.numpy as jnp
from jax import lax
from jax.experimental import pallas as pl
from jax.experimental.pallas import tpu as pltpu
from jax.sharding import PartitionSpec as P

CI = 256
C = 512
TE = 128
KW = 5
H = 16
HD = 8
KD = 3
NSMALL = 10
STEP = 10
BLK = 128
COND = 1152
NBLK = 62
GC = 64

FIRST_AT, FIRST_N = 0, 10
SECOND_AT, SECOND_N = 10, 20
RES_AT, RES_N = 30, 2
DOWN_AT, DOWN_N = 32, 12
SCALE_AT, SHIFT_AT, FILM_N = 44, 53, 9

BETA_ONE = 0.9
BETA_TWO = 0.999
EPS_ADAM = 1e-08
DECAY = 0.01
RATE_MATRIX = 0.1
RATE_SMALL = 1.0

F32 = jnp.float32
BF = jnp.bfloat16
NT = (((1,), (1,)), ((), ()))
TN = (((0,), (0,)), ((), ()))
VMEM_LIMIT = 56 * 2**20


def mish(value):
    return value * jnp.tanh(jax.nn.softplus(value))


def time_embed(step_ids, width):
    half = width // 2
    freq = jnp.exp(-math.log(10000.0) * jnp.arange(half, dtype=F32) / (half - 1))
    angle = step_ids.astype(F32)[:, None] * freq[None, :]
    return jnp.concatenate([jnp.sin(angle), jnp.cos(angle)], axis=1)


def slot_of(owners, slot_count):
    same = owners[:, None] == owners[None, :]
    order = jnp.arange(owners.shape[0], dtype=jnp.int32)
    earlier = order[:, None] > order[None, :]
    rank = jnp.sum((same & earlier).astype(jnp.int32), axis=1)
    return owners * slot_count + rank


def adamw(weight, first_m, second_m, grad, rate):
    first_new = BETA_ONE * first_m + (1.0 - BETA_ONE) * grad
    second_new = BETA_TWO * second_m + (1.0 - BETA_TWO) * grad * grad
    fix_one = 1.0 - BETA_ONE**STEP
    fix_two = 1.0 - BETA_TWO**STEP
    update = first_new / fix_one / (jnp.sqrt(second_new / fix_two) + EPS_ADAM) + DECAY * weight
    return (first_new, second_new, weight - rate * update)


def recip(value):
    r = pl.reciprocal(value, approx=True)
    return r * (2.0 - value * r)


def mish_parts(v):
    w = jnp.exp(jnp.minimum(v, 30.0))
    n = w * (w + 2.0)
    r = recip(n + 2.0)
    return w, n * r, r


def mish_only(v):
    _, t, _ = mish_parts(v)
    return v * t


def mish_both(v):
    w, t, r = mish_parts(v)
    return v * t, t + (4.0 * v) * (((w * (1.0 + w)) * r) * r)


def group_sum(value):
    low_half = lax.broadcasted_iota(jnp.int32, value.shape, 1) < GC
    zero = jnp.zeros_like(value)
    left = jnp.sum(jnp.where(low_half, value, zero), axis=1, keepdims=True)
    right = jnp.sum(jnp.where(low_half, zero, value), axis=1, keepdims=True)
    return jnp.where(low_half, left, right)


def lanes(q):
    return slice(q * 128, (q + 1) * 128)


def fetch(w_hbm, at, count, dst, sem, k):
    return [
        pltpu.make_async_copy(w_hbm.at[p, at : at + count], dst.at[:, p], sem.at[k, p])
        for p in range(4)
    ]


def begin(copies):
    for copy in copies:
        copy.start()


def finish(copies):
    for copy in copies:
        copy.wait()


def matrix(ref, at, count):
    return ref[at : at + count].reshape(count * BLK, C)


def first_kernel(w_hbm, x_ref, cond_ref, lens_ref, inv_ref, small_ref, normed_ref, rstd_ref, hid_ref, mod_ref,
                 w_one, w_film, xp, fst, sem):
    step = pl.program_id(0)
    frames, width, _ = x_ref.shape
    rows = frames * width

    @pl.when(step == 0)
    def _():
        film = fetch(w_hbm, SCALE_AT, 2 * FILM_N, w_film, sem, 0)
        one = fetch(w_hbm, FIRST_AT, FIRST_N, w_one, sem, 1)
        begin(film)
        begin(one)
        xp[0:2] = jnp.zeros((2, width, CI), BF)
        xp[frames + 2 :] = jnp.zeros((2, width, CI), BF)
        finish(film)
        for k in range(2):
            mod_ref[k] = (
                jnp.dot(cond_ref[...], matrix(w_film, k * FILM_N, FILM_N), preferred_element_type=F32)
                + small_ref[3 + k : 4 + k]
            )
        finish(one)

    xp[2 : frames + 2] = x_ref[...]
    acc = jnp.dot(xp[0:frames].reshape(rows, CI), matrix(w_one, 0, 2), preferred_element_type=F32)
    for a in range(1, KW):
        acc = acc + jnp.dot(
            xp[a : a + frames].reshape(rows, CI), matrix(w_one, 2 * a, 2), preferred_element_type=F32
        )
    fst[...] = (acc + small_ref[0:1]).reshape(frames, width, C)

    here = pl.ds(pl.multiple_of(step * width, width), width)
    lens = lens_ref[...]
    inv = inv_ref[...]
    for q in range(C // 128):
        ls = lanes(q)
        total = jnp.zeros((width, 128), F32)
        for t in range(frames):
            total = total + jnp.where(lens > t, fst[t, :, ls], 0.0)
        mean = group_sum(total) * inv
        total = jnp.zeros((width, 128), F32)
        for t in range(frames):
            centered = fst[t, :, ls] - mean
            total = total + jnp.where(lens > t, centered * centered, 0.0)
        rstd = lax.rsqrt(group_sum(total) * inv + 1e-05)
        rstd_ref[:, ls] = rstd
        gain, bias = small_ref[1:2, ls], small_ref[2:3, ls]
        scale, shift = mod_ref[0, here, ls], mod_ref[1, here, ls]
        for t in range(frames):
            normed = (fst[t, :, ls] - mean) * rstd
            normed_ref[t, :, ls] = normed
            value = scale * mish_only(normed * gain + bias) + shift
            hid_ref[t, :, ls] = jnp.where(lens > t, value, 0.0).astype(BF)


def second_kernel(w_hbm, hid_ref, x_ref, cs_ref, cd_ref, lens_ref, inv_ref, small_ref, skip_ref, dskip_ref, g2_ref,
                  gw_ref, gs_ref, w_two, w_res, w_down, hp, cdp, sec, br, dev, dod, se, so, acc, sem):
    step = pl.program_id(0)
    last = pl.num_programs(0) - 1
    frames, width, _ = x_ref.shape
    half = frames // 2
    rows = frames * width

    @pl.when(step == 0)
    def _():
        down = fetch(w_hbm, DOWN_AT, DOWN_N, w_down, sem, 0)
        res = fetch(w_hbm, RES_AT, RES_N, w_res, sem, 1)
        two = fetch(w_hbm, SECOND_AT, SECOND_N, w_two, sem, 2)
        begin(down)
        begin(res)
        begin(two)
        hp[0:2] = jnp.zeros((2, width, C), BF)
        hp[frames + 2 :] = jnp.zeros((2, width, C), BF)
        cdp[half:] = jnp.zeros((1, width, C), BF)
        so[0:1] = jnp.zeros((1, width, C), BF)
        acc[...] = jnp.zeros_like(acc)
        gs_ref[...] = jnp.zeros_like(gs_ref)
        finish(down)
        finish(res)
        finish(two)

    hp[2 : frames + 2] = hid_ref[...]
    cdp[0:half] = cd_ref[...]
    cot = cdp[0:half].reshape(half * width, C)
    cot_next = cdp[1 : half + 1].reshape(half * width, C)
    dev[...] = lax.dot_general(cot, matrix(w_down, 4, 4), NT, preferred_element_type=F32).reshape(half, width, C)
    dod[...] = (
        lax.dot_general(cot, matrix(w_down, 8, 4), NT, preferred_element_type=F32)
        + lax.dot_general(cot_next, matrix(w_down, 0, 4), NT, preferred_element_type=F32)
    ).reshape(half, width, C)
    br[...] = (
        jnp.dot(x_ref[...].reshape(rows, CI), matrix(w_res, 0, 2), preferred_element_type=F32) + small_ref[8:9]
    ).reshape(frames, width, C)
    total = jnp.dot(hp[0:frames].reshape(rows, C), matrix(w_two, 0, 4), preferred_element_type=F32)
    for a in range(1, KW):
        total = total + jnp.dot(
            hp[a : a + frames].reshape(rows, C), matrix(w_two, 4 * a, 4), preferred_element_type=F32
        )
    sec[...] = (total + small_ref[5:6]).reshape(frames, width, C)

    lens = lens_ref[...]
    inv = inv_ref[...]
    zero = jnp.zeros((width, 128), F32)
    for q in range(C // 128):
        ls = lanes(q)
        total = zero
        for t in range(frames):
            total = total + jnp.where(lens > t, sec[t, :, ls], 0.0)
        mean = group_sum(total) * inv
        total = zero
        for t in range(frames):
            centered = sec[t, :, ls] - mean
            total = total + jnp.where(lens > t, centered * centered, 0.0)
        rstd = lax.rsqrt(group_sum(total) * inv + 1e-05)
        gain, bias = small_ref[6:7, ls], small_ref[7:8, ls]
        sum_dy, sum_dyn, sum_ds = zero, zero, zero
        for t in range(frames):
            normed = (sec[t, :, ls] - mean) * rstd
            sec[t, :, ls] = normed
            act, slope = mish_both(normed * gain + bias)
            skip = (act + br[t, :, ls]).astype(BF)
            skip_ref[t, :, ls] = skip
            if t % 2:
                so[t // 2 + 1, :, ls] = skip
                back = dod[t // 2, :, ls]
            else:
                se[t // 2, :, ls] = skip
                back = dev[t // 2, :, ls]
            ds = (cs_ref[t, :, ls].astype(F32) + back).astype(BF)
            dskip_ref[t, :, ls] = ds
            ds = ds.astype(F32)
            sum_ds = sum_ds + ds
            dy = ds * slope
            br[t, :, ls] = dy
            sum_dy = sum_dy + dy
            sum_dyn = sum_dyn + dy * normed
        mean_a = group_sum(sum_dy * gain) * inv
        mean_an = group_sum(sum_dyn * gain) * inv
        sum_g, sum_cd = zero, zero
        for t in range(frames):
            normed = sec[t, :, ls]
            grad = rstd * (br[t, :, ls] * gain - jnp.where(lens > t, mean_a + normed * mean_an, 0.0))
            grad = grad.astype(BF)
            g2_ref[t, :, ls] = grad
            sum_g = sum_g + grad.astype(F32)
        for t in range(half):
            sum_cd = sum_cd + cd_ref[t, :, ls].astype(F32)
        for k, part in enumerate((sum_g, sum_dyn, sum_dy, sum_ds, sum_cd)):
            gs_ref[k : k + 1, ls] += jnp.sum(part, axis=0, keepdims=True)

    grad_two = g2_ref[...].reshape(rows, C)
    for a in range(KW):
        acc[a * C : (a + 1) * C] += lax.dot_general(
            hp[a : a + frames].reshape(rows, C), grad_two, TN, preferred_element_type=F32
        )
    at = KW * C
    acc[at : at + CI] += lax.dot_general(
        x_ref[...].reshape(rows, CI), dskip_ref[...].reshape(rows, C), TN, preferred_element_type=F32
    )
    at = at + CI
    for a, source in enumerate((so.at[0:half], se, so.at[1 : half + 1])):
        acc[at + a * C : at + (a + 1) * C] += lax.dot_general(
            source[...].reshape(half * width, C), cot, TN, preferred_element_type=F32
        )

    @pl.when(step == last)
    def _():
        for b in range(acc.shape[0] // BLK):
            for p in range(4):
                at = b * BLK + p * 32
                gw_ref[p, b] = acc[at : at + 32].astype(BF)


def third_kernel(w_hbm, g2_ref, x_ref, cond_ref, normed_ref, rstd_ref, mod_ref, lens_ref, inv_ref, small_ref,
                 g1_ref, dmod_ref, gw_ref, gs_ref, w_two, gp, xp, dh, acc, sem):
    step = pl.program_id(0)
    last = pl.num_programs(0) - 1
    frames, width, _ = x_ref.shape
    rows = frames * width

    @pl.when(step == 0)
    def _():
        two = fetch(w_hbm, SECOND_AT, SECOND_N, w_two, sem, 0)
        begin(two)
        gp[0:2] = jnp.zeros((2, width, C), BF)
        gp[frames + 2 :] = jnp.zeros((2, width, C), BF)
        xp[0:2] = jnp.zeros((2, width, CI), BF)
        xp[frames + 2 :] = jnp.zeros((2, width, CI), BF)
        acc[...] = jnp.zeros_like(acc)
        gs_ref[...] = jnp.zeros_like(gs_ref)
        finish(two)

    gp[2 : frames + 2] = g2_ref[...]
    xp[2 : frames + 2] = x_ref[...]
    total = lax.dot_general(gp[4 : 4 + frames].reshape(rows, C), matrix(w_two, 0, 4), NT, preferred_element_type=F32)
    for a in range(1, KW):
        total = total + lax.dot_general(
            gp[4 - a : 4 - a + frames].reshape(rows, C), matrix(w_two, 4 * a, 4), NT, preferred_element_type=F32
        )
    dh[...] = total.reshape(frames, width, C)

    here = pl.ds(pl.multiple_of(step * width, width), width)
    lens = lens_ref[...]
    inv = inv_ref[...]
    zero = jnp.zeros((width, 128), F32)
    for q in range(C // 128):
        ls = lanes(q)
        gain, bias = small_ref[1:2, ls], small_ref[2:3, ls]
        scale = mod_ref[0, here, ls]
        sum_dy, sum_dyn, d_scale, d_shift = zero, zero, zero, zero
        for t in range(frames):
            normed = normed_ref[t, :, ls]
            act, slope = mish_both(normed * gain + bias)
            grad = jnp.where(lens > t, dh[t, :, ls], 0.0)
            d_scale = d_scale + grad * act
            d_shift = d_shift + grad
            dy = (grad * scale) * slope
            dh[t, :, ls] = dy
            sum_dy = sum_dy + dy
            sum_dyn = sum_dyn + dy * normed
        mean_a = group_sum(sum_dy * gain) * inv
        mean_an = group_sum(sum_dyn * gain) * inv
        rstd = rstd_ref[:, ls]
        sum_g = zero
        for t in range(frames):
            normed = normed_ref[t, :, ls]
            grad = rstd * (dh[t, :, ls] * gain - jnp.where(lens > t, mean_a + normed * mean_an, 0.0))
            grad = grad.astype(BF)
            g1_ref[t, :, ls] = grad
            sum_g = sum_g + grad.astype(F32)
        d_scale, d_shift = d_scale.astype(BF), d_shift.astype(BF)
        dmod_ref[0, here, ls] = d_scale
        dmod_ref[1, here, ls] = d_shift
        for k, part in enumerate((sum_g, sum_dyn, sum_dy, d_scale.astype(F32), d_shift.astype(F32))):
            gs_ref[k : k + 1, ls] += jnp.sum(part, axis=0, keepdims=True)

    grad_one = g1_ref[...].reshape(rows, C)
    for a in range(KW):
        acc[a * CI : (a + 1) * CI] += lax.dot_general(
            xp[a : a + frames].reshape(rows, CI), grad_one, TN, preferred_element_type=F32
        )

    @pl.when(step == last)
    def _():
        for b in range(FIRST_N):
            for p in range(4):
                at = b * BLK + p * 32
                gw_ref[p, b] = acc[at : at + 32].astype(BF)
        for k in range(2):
            film = lax.dot_general(cond_ref[...], dmod_ref[k], TN, preferred_element_type=F32).astype(BF)
            for b in range(FILM_N):
                for p in range(4):
                    at = b * BLK + p * 32
                    gw_ref[p, FIRST_N + k * FILM_N + b] = film[at : at + 32]


def fourth_kernel(w_hbm, skip_ref, g1_ref, dskip_ref, dmod_ref, slope_ref, lens_ref, small_ref, down_ref, dx_ref,
                  dobs_ref, w_one, w_res, w_down, w_film, gp, se, so, sem):
    step = pl.program_id(0)
    frames, width, _ = skip_ref.shape
    half = frames // 2
    rows = frames * width

    @pl.when(step == 0)
    def _():
        film = fetch(w_hbm, SCALE_AT, 2 * FILM_N, w_film, sem, 0)
        one = fetch(w_hbm, FIRST_AT, FIRST_N, w_one, sem, 1)
        res = fetch(w_hbm, RES_AT, RES_N, w_res, sem, 2)
        down = fetch(w_hbm, DOWN_AT, DOWN_N, w_down, sem, 3)
        begin(film)
        begin(one)
        begin(res)
        begin(down)
        gp[0:2] = jnp.zeros((2, width, C), BF)
        gp[frames + 2 :] = jnp.zeros((2, width, C), BF)
        so[0:1] = jnp.zeros((1, width, C), BF)
        finish(film)
        back = lax.dot_general(dmod_ref[0], matrix(w_film, 1, FILM_N - 1), NT, preferred_element_type=F32)
        back = back + lax.dot_general(
            dmod_ref[1], matrix(w_film, FILM_N + 1, FILM_N - 1), NT, preferred_element_type=F32
        )
        dobs_ref[...] = back * slope_ref[...]
        finish(one)
        finish(res)
        finish(down)

    gp[2 : frames + 2] = g1_ref[...]
    total = lax.dot_general(dskip_ref[...].reshape(rows, C), matrix(w_res, 0, 2), NT, preferred_element_type=F32)
    for a in range(KW):
        total = total + lax.dot_general(
            gp[4 - a : 4 - a + frames].reshape(rows, C), matrix(w_one, 2 * a, 2), NT, preferred_element_type=F32
        )
    total = total.reshape(frames, width, CI)
    lens = lens_ref[...]
    for t in range(frames):
        for q in range(CI // 128):
            dx_ref[t, :, lanes(q)] = jnp.where(lens > t, total[t, :, lanes(q)], 0.0)
    for j in range(half):
        se[j] = skip_ref[2 * j]
        so[j + 1] = skip_ref[2 * j + 1]
    down = jnp.dot(so[0:half].reshape(half * width, C), matrix(w_down, 0, 4), preferred_element_type=F32)
    down = down + jnp.dot(se[...].reshape(half * width, C), matrix(w_down, 4, 4), preferred_element_type=F32)
    down = down + jnp.dot(
        so[1 : half + 1].reshape(half * width, C), matrix(w_down, 8, 4), preferred_element_type=F32
    )
    down_ref[...] = (down + small_ref[9:10]).astype(BF).reshape(half, width, C)


def tiles(frames, width, channels):
    return pl.BlockSpec((frames, width, channels), lambda i: (0, i, 0))


def rows_of(width, channels):
    return pl.BlockSpec((width, channels), lambda i: (i, 0))


def whole(*shape):
    return pl.BlockSpec(shape, lambda i: (0,) * len(shape))


ANY = pl.BlockSpec(memory_space=pl.ANY)
PARAMS = pltpu.CompilerParams(vmem_limit_bytes=VMEM_LIMIT, dimension_semantics=("arbitrary",))


def weight_scratch(count):
    return pltpu.VMEM((count, 4, 32, C), BF)


def shape(*dims, dtype=F32):
    return jax.ShapeDtypeStruct(dims, dtype)


def run_first(weights, x, cond, lens, inv, small, width):
    count = x.shape[1]
    return pl.pallas_call(
        first_kernel,
        grid=(count // width,),
        in_specs=[ANY, tiles(H, width, CI), whole(count, COND), rows_of(width, 128), rows_of(width, 128),
                  whole(NSMALL, C)],
        out_specs=[tiles(H, width, C), rows_of(width, C), tiles(H, width, C), whole(2, count, C)],
        out_shape=[shape(H, count, C), shape(count, C), shape(H, count, C, dtype=BF), shape(2, count, C)],
        scratch_shapes=[weight_scratch(FIRST_N), weight_scratch(2 * FILM_N), pltpu.VMEM((H + 4, width, CI), BF),
                        pltpu.VMEM((H, width, C), F32), pltpu.SemaphoreType.DMA((2, 4))],
        compiler_params=PARAMS,
        name="first",
    )(weights, x, cond, lens, inv, small)


def run_second(weights, hid, x, cs, cd, lens, inv, small, width):
    count = x.shape[1]
    blocks = SECOND_N + RES_N + DOWN_N
    return pl.pallas_call(
        second_kernel,
        grid=(count // width,),
        in_specs=[ANY, tiles(H, width, C), tiles(H, width, CI), tiles(H, width, C), tiles(HD, width, C),
                  rows_of(width, 128), rows_of(width, 128), whole(NSMALL, C)],
        out_specs=[tiles(H, width, C), tiles(H, width, C), tiles(H, width, C), whole(4, blocks, 32, C), whole(8, C)],
        out_shape=[shape(H, count, C, dtype=BF)] * 3 + [shape(4, blocks, 32, C, dtype=BF), shape(8, C)],
        scratch_shapes=[weight_scratch(SECOND_N), weight_scratch(RES_N), weight_scratch(DOWN_N),
                        pltpu.VMEM((H + 4, width, C), BF), pltpu.VMEM((HD + 1, width, C), BF),
                        pltpu.VMEM((H, width, C), F32), pltpu.VMEM((H, width, C), F32),
                        pltpu.VMEM((HD, width, C), F32), pltpu.VMEM((HD, width, C), F32),
                        pltpu.VMEM((HD, width, C), BF), pltpu.VMEM((HD + 1, width, C), BF),
                        pltpu.VMEM((blocks * BLK, C), F32), pltpu.SemaphoreType.DMA((3, 4))],
        compiler_params=PARAMS,
        name="second",
    )(weights, hid, x, cs, cd, lens, inv, small)


def run_third(weights, g2, x, cond, normed, rstd, mod, lens, inv, small, width):
    count = x.shape[1]
    blocks = FIRST_N + 2 * FILM_N
    return pl.pallas_call(
        third_kernel,
        grid=(count // width,),
        in_specs=[ANY, tiles(H, width, C), tiles(H, width, CI), whole(count, COND), tiles(H, width, C),
                  rows_of(width, C), whole(2, count, C), rows_of(width, 128), rows_of(width, 128), whole(NSMALL, C)],
        out_specs=[tiles(H, width, C), whole(2, count, C), whole(4, blocks, 32, C), whole(8, C)],
        out_shape=[shape(H, count, C, dtype=BF), shape(2, count, C, dtype=BF), shape(4, blocks, 32, C, dtype=BF),
                   shape(8, C)],
        scratch_shapes=[weight_scratch(SECOND_N), pltpu.VMEM((H + 4, width, C), BF),
                        pltpu.VMEM((H + 4, width, CI), BF), pltpu.VMEM((H, width, C), F32),
                        pltpu.VMEM((FIRST_N * BLK, C), F32), pltpu.SemaphoreType.DMA((1, 4))],
        compiler_params=PARAMS,
        name="third",
    )(weights, g2, x, cond, normed, rstd, mod, lens, inv, small)


def run_fourth(weights, skip, g1, dskip, dmod, slope, lens, small, width):
    count = skip.shape[1]
    features = slope.shape[1]
    return pl.pallas_call(
        fourth_kernel,
        grid=(count // width,),
        in_specs=[ANY, tiles(H, width, C), tiles(H, width, C), tiles(H, width, C), whole(2, count, C),
                  whole(count, features), rows_of(width, 128), whole(NSMALL, C)],
        out_specs=[tiles(HD, width, C), tiles(H, width, CI), whole(count, features)],
        out_shape=[shape(HD, count, C, dtype=BF), shape(H, count, CI), shape(count, features)],
        scratch_shapes=[weight_scratch(FIRST_N), weight_scratch(RES_N), weight_scratch(DOWN_N),
                        weight_scratch(2 * FILM_N), pltpu.VMEM((H + 4, width, C), BF),
                        pltpu.VMEM((HD, width, C), BF), pltpu.VMEM((HD + 1, width, C), BF),
                        pltpu.SemaphoreType.DMA((4, 4))],
        compiler_params=PARAMS,
        name="fourth",
    )(weights, skip, g1, dskip, dmod, slope, lens, small)


def local_work(weights, actions, shared, tsteps, lengths, cot_skip, cot_down, small_master):
    micro, samp = lengths.shape
    count = micro * samp
    lens_flat = lengths.reshape(count)
    lens = jnp.broadcast_to(lens_flat.astype(F32)[:, None], (count, 128))
    inv = 1.0 / (lens * GC)
    keep = jnp.arange(H)[:, None, None] < lens_flat[None, :, None]
    x = jnp.where(keep, actions.reshape(count, H, CI).transpose(1, 0, 2), jnp.zeros((), BF))
    cs = cot_skip.reshape(count, H, C).transpose(1, 0, 2)
    cd = cot_down.reshape(count, HD, C).transpose(1, 0, 2)
    obs = shared.reshape(count, -1).astype(F32)
    obs_act, obs_back = jax.vjp(mish, obs)
    slope = obs_back(jnp.ones_like(obs))[0]
    cond = jnp.concatenate([mish(time_embed(tsteps.reshape(count), TE)), obs_act], axis=1).astype(BF)

    width = samp
    normed, rstd, hid, mod = run_first(weights, x, cond, lens, inv, small_master, width)
    skip, dskip, g2, gw_late, gs_late = run_second(weights, hid, x, cs, cd, lens, inv, small_master, width)
    g1, dmod, gw_early, gs_early = run_third(
        weights, g2, x, cond, normed, rstd, mod, lens, inv, small_master, width
    )
    down, dx, dobs = run_fourth(weights, skip, g1, dskip, dmod, slope, lens, small_master, width)
    skip_out = skip.transpose(1, 0, 2).reshape(micro, samp, H, C)
    down_out = down.transpose(1, 0, 2).reshape(micro, samp, HD, C)
    actions_grad = dx.transpose(1, 0, 2).reshape(micro, samp, H, CI)
    obs_local = dobs.reshape(micro, samp, -1)
    g_small = jnp.concatenate(
        [gs_early[0:5], gs_late[0:5]], axis=0
    )
    return skip_out, down_out, actions_grad, obs_local, gw_early, gw_late, g_small


def body(
    actions,
    observations,
    tsteps,
    lengths,
    cot_skip,
    cot_down,
    owners,
    master,
    moment_one,
    moment_two,
    small_master,
    small_one,
    small_two,
):
    slot_count = master.shape[0]
    dp_count = lax.axis_size("dp")
    slots_all = dp_count * slot_count
    me_pair = lax.axis_index("pair")
    me_dp = lax.axis_index("dp")
    slot_index = slot_of(owners, slot_count)
    block_of = (
        jnp.full((slots_all,), -1, jnp.int32).at[slot_index].set(jnp.arange(NBLK, dtype=jnp.int32))
    )
    quarter = lax.dynamic_slice_in_dim(master, me_pair * 32, 32, axis=1).astype(BF)
    slots = lax.all_gather(quarter, "dp", axis=0, tiled=True)
    mine = jnp.take(slots, slot_index, axis=0)
    weights = lax.all_gather(mine, "pair", axis=0)
    shared = lax.all_gather(observations, "pair", axis=2, tiled=True)

    skip_out, down_out, actions_grad, obs_local, gw_early, gw_late, g_small = local_work(
        weights, actions, shared, tsteps, lengths, cot_skip, cot_down, small_master
    )

    late = lax.psum_scatter(gw_late, "pair", scatter_dimension=0)
    early = lax.psum_scatter(gw_early, "pair", scatter_dimension=0)
    grad_small = lax.psum(g_small, ("dp", "pair"))
    observations_grad = lax.psum_scatter(obs_local, "pair", scatter_dimension=2, tiled=True)
    grads = jnp.concatenate([early[:FIRST_N], late, early[FIRST_N:]], axis=0)
    spread = jnp.take(grads, jnp.maximum(block_of, 0), axis=0)
    owned = lax.psum_scatter(spread, "dp", scatter_dimension=0, tiled=True)
    owned = lax.all_gather(owned, "pair", axis=1, tiled=True)
    used = lax.dynamic_slice_in_dim(block_of, me_dp * slot_count, slot_count, axis=0) >= 0
    owned = jnp.where(used[:, None, None], owned.astype(F32), 0.0)
    new_one, new_two, new_master = adamw(master, moment_one, moment_two, owned, RATE_MATRIX)
    small_first, small_second, new_small = adamw(
        small_master, small_one, small_two, grad_small, RATE_SMALL
    )
    return (
        skip_out,
        down_out,
        actions_grad,
        observations_grad,
        new_one,
        new_two,
        new_master,
        small_first,
        small_second,
        new_small,
    )


def solution(mesh):
    placed = (
        P(None, ("dp", "pair"), None, None),
        P(None, "dp", "pair"),
        P(None, ("dp", "pair")),
        P(None, ("dp", "pair")),
        P(None, ("dp", "pair"), None, None),
        P(None, ("dp", "pair"), None, None),
        P(),
        P("dp", None, None),
        P("dp", None, None),
        P("dp", None, None),
        P(),
        P(),
        P(),
    )
    return jax.shard_map(
        body,
        mesh=mesh,
        in_specs=placed,
        out_specs=(
            P(None, ("dp", "pair"), None, None),
            P(None, ("dp", "pair"), None, None),
            P(None, ("dp", "pair"), None, None),
            P(None, "dp", "pair"),
            P("dp", None, None),
            P("dp", None, None),
            P("dp", None, None),
            P(),
            P(),
            P(),
        ),
        check_vma=False,
    )
```

time: 1950 us -> 510 us (0.26)
  waiting for transfers between devices: 883 us -> 285 us
  local copies, waits for them, and re-layouts: 470 us -> 32.4 us
  other arithmetic: 371 us -> 24.7 us
  matrix products: 143 us -> 0 us
  Pallas kernels: 0 us -> 102 us
    reduce_scatter x1 -> x3, waiting for transfers between devices: 501 us -> 175 us  [the longest x1 88.2 us: body(): owned = lax.psum_scatter(spread, 'dp', scatter_dimension=0, tiled=True)]
    reduce_sum x72 -> x0, other arithmetic: 175 us -> none  [the longest x12 35.2 us: group_norm(): normed = centered * lax.rsqrt(var + 1e-05)[:, None, :, None]]
    scatter-add x40 -> x0, local copies, waits for them, and re-layouts: 174 us -> none  [fold_taps(): total.at[:, tap_index:tap_index + stride * (count - 1) + 1:stride]]
    psum x1 -> x0, waiting for transfers between devices: 147 us -> none  [body(): lax.psum(grad_rows.astype(jnp.bfloat16), 'pair').astype(jnp.float32)]
    dot_general x60 -> x0, matrix products: 143 us -> none  [the longest x20 73.5 us: weight_grad(): jnp.einsum('nk,nc->kc', cols, grads, preferred_element_type=jnp.float32)]
    all_gather x1 -> x3, waiting for transfers between devices: 221 us -> 110 us  [the longest x1 75.8 us: body(): slots = lax.all_gather(quarter, 'dp', axis=0, tiled=True)]
    pallas_call x0 -> x4, Pallas kernels: none -> 102 us  [the longest x1 42.7 us: run_second(): pl.pallas_call(second_kernel, grid=(count // width,), in_specs=[ANY, tile...]
    add x44 -> x0, other arithmetic: 72.5 us -> none  [the longest x40 72.5 us: fold_taps(): total.at[:, tap_index:tap_index + stride * (count - 1) + 1:stride]]
  transfers between devices with their start and end apart: 4 -> 7, of which waited for: 4 -> 5; matrix products, arithmetic and copies ran while one was open for 1% -> 8% of each run, Pallas kernels for 0% -> 3%
where the time goes in v1:
time: 510 us; the launch traced here: 509 us
  waiting for transfers between devices  285 us (56%)
  Pallas kernels  102 us (20%)
  blocking collectives  49.4 us (10%)
  local copies, waits for them, and re-layouts  32.4 us (6%)
  other arithmetic  24.7 us (5%)
  between operations  14.4 us (3%)
    reduce_scatter x1, waiting for transfers between devices, body(): owned = lax.psum_scatter(spread, 'dp', scatter_dimension=0, tiled=True)  88.2 us
    all_gather x1, waiting for transfers between devices, body(): slots = lax.all_gather(quarter, 'dp', axis=0, tiled=True)  75.8 us
    reduce_scatter x1, waiting for transfers between devices, body(): late = lax.psum_scatter(gw_late, 'pair', scatter_dimension=0)  46.7 us
    pallas_call x1, Pallas kernels, run_second(): pl.pallas_call(second_kernel, grid=(count // width,), in_specs=[ANY, tile...  42.7 us
    psum x1, blocking collectives, body(): grad_small = lax.psum(g_small, ('dp', 'pair'))  40.4 us
    reduce_scatter x1, waiting for transfers between devices, body(): early = lax.psum_scatter(gw_early, 'pair', scatter_dimension=0)  39.9 us
    all_gather x1, waiting for transfers between devices, body(): weights = lax.all_gather(mine, 'pair', axis=0)  34.2 us
    pallas_call x1, Pallas kernels, run_third(): pl.pallas_call(third_kernel, grid=(count // width,), in_specs=[ANY, tiles...  29.2 us
  transfers between devices with their start and end apart: 7, of which 5 were waited for; matrix products, arithmetic and copies ran while one was open for 8% of the time, Pallas kernels for 3%

profile of v1, /device:TPU:0, one launch (start us, length us, event | category | flops | bytes accessed | tf_op | source)
XLA Modules:
  0.0 509.0 jit_solution(14045058307483158696)
XLA Ops:
  7.2 2.1 dynamic-slice_convert_fusion
  9.4 0.9 convert_reduce_fusion
  11.0 75.8 %all-gather.4.cloned.1.call-done = bf16[128,32,512]{2,1,0:T(8,128)(2,1)} async-done(((bf16[16,32,512]{2,1,0:T(8,128)(2,1)}), bf16[128,32,512]{2,1,0:T(8,128)(2,1)}) %all-gather.4.cloned.1.call-update) | async-done | bytes 4194320 | tf_op jit(solution)/shard_map/all_gather | solution.py:591
  86.8 2.9 gather_fusion
  89.7 1.5 bitcast_select_fusion
  91.5 2.1 copy.35
  93.6 5.4 %copy.36 = bf16[4,48,16,512]{3,1,0,2:T(8,128)(2,1)} copy(bf16[4,48,16,512]{3,2,1,0:T(8,128)(2,1)} %param.17) | data formatting | bytes 6291456 | tf_op args[4]
  99.0 1.6 copy.37
  101.2 9.0 %all_gather.15 = bf16[4,48,1024]{2,1,0:T(8,128)(2,1)S(1)} all-gather(bf16[4,48,256]{2,1,0:T(8,128)(2,1)S(1)} %copy-done.4), channel_id=1, replica_groups=mesh['dp'=8,'pair'=4] {'pair'}, dimensions={2}, use_global_device_ids=true | all-gather | bytes 491520 | tf_op jit(solution)/shard_map/all_gather | solution.py:594
  110.3 1.8 fusion.7
  112.0 0.8 pad_maximum_fusion.1.cond_ref
  112.8 1.6 bitcast_select_fusion.1.x_ref
  114.4 34.2 %all-gather.6.cloned.1.call-done.w_hbm = bf16[4,62,32,512]{3,2,1,0:T(8,128)(2,1)} async-done(((bf16[1,62,32,512]{3,2,1,0:T(8,128)(2,1)}), bf16[4,62,32,512]{3,2,1,0:T(8,128)(2,1)}) %all-gather.6.cloned.1.call-update) | async-done | bytes 8126480 | tf_op jit(solution)/shard_map/all_gather | solution.py:593
  149.4 0.7 broadcast_in_dim.74.inv_ref
  150.1 15.7 %first.1 = (f32[16,192,512]{2,1,0:T(8,128)}, f32[192,512]{1,0:T(8,128)}, bf16[16,192,512]{2,1,0:T(8,128)(2,1)}, f32[2,192,512]{2,1,0:T(8,128)}) custom-call(bf16[4,62,32,512]{3,2,1,0:T(8,128)(2,1)} %all-gather.6.cloned.1.call-done.w_hbm, bf16[16,192,256]{2,1,0:T(8,128)(2,1)} %bitcast_select_fusion.1.x_ref, bf16[192,1152]{1,0:T(8,128)(2,1)} %pad_maximum_fusion.1.cond_ref, ...), custom_call_target="tpu_custom_call" | custom-call | tf_op jit(solution)/shard_map/first/pallas_call | solution.py:461
  165.8 42.7 %second.1 = (bf16[16,192,512]{2,1,0:T(8,128)(2,1)}, bf16[16,192,512]{2,1,0:T(8,128)(2,1)}, bf16[16,192,512]{2,1,0:T(8,128)(2,1)}, bf16[4,34,32,512]{3,2,1,0:T(8,128)(2,1)}, f32[8,512]{1,0:T(8,128)}) custom-call(bf16[4,62,32,512]{3,2,1,0:T(8,128)(2,1)} %all-gather.6.cloned.1.call-done.w_hbm, bf16[16,192,512]{2,1,0:T(8,128)(2,1)} %get-tuple-element.26.hid_ref, ...), custom_call_target="tpu_custom_call" | custom-call | tf_op jit(solution)/shard_map/second/pallas_call | solution.py:478
  208.6 29.2 %third.1 = (bf16[16,192,512]{2,1,0:T(8,128)(2,1)}, bf16[2,192,512]{2,1,0:T(8,128)(2,1)}, bf16[4,28,32,512]{3,2,1,0:T(8,128)(2,1)}, f32[8,512]{1,0:T(8,128)}) custom-call(bf16[4,62,32,512]{3,2,1,0:T(8,128)(2,1)} %all-gather.6.cloned.1.call-done.w_hbm, bf16[16,192,512]{2,1,0:T(8,128)(2,1)} %get-tuple-element.28.g2_ref, ...), custom_call_target="tpu_custom_call" | custom-call | tf_op jit(solution)/shard_map/third/pallas_call | solution.py:499
  238.4 0.8 scatter_custom_fusion
  239.2 39.9 %reduce-scatter.7.cloned.1.call-done = bf16[1,28,32,512]{3,2,1,0:T(8,128)(2,1)} async-done(((bf16[4,28,32,512]{3,2,1,0:T(8,128)(2,1)}), bf16[1,28,32,512]{3,2,1,0:T(8,128)(2,1)}) %reduce-scatter.7.cloned.1.call-update) | async-done | bytes 917520 | tf_op jit(solution)/shard_map/reduce_scatter | solution.py:601
  279.2 1.0 slice_bitcast_fusion.1
  280.2 1.1 slice_bitcast_fusion
  281.3 46.7 %reduce-scatter.9.cloned.1.call-done = bf16[1,34,32,512]{3,2,1,0:T(8,128)(2,1)} async-done(((bf16[4,34,32,512]{3,2,1,0:T(8,128)(2,1)}), bf16[1,34,32,512]{3,2,1,0:T(8,128)(2,1)}) %reduce-scatter.9.cloned.1.call-update) | async-done | bytes 1114128 | tf_op jit(solution)/shard_map/reduce_scatter | solution.py:600
  327.9 1.5 pad_maximum_fusion
  329.4 2.8 gather_fusion.1
  332.2 4.6 broadcast_select_fusion
  336.9 88.2 %reduce-scatter.11.cloned.1.call-done = bf16[16,32,512]{2,1,0:T(8,128)(2,1)} async-done(((bf16[128,32,512]{2,1,0:T(8,128)(2,1)}), bf16[16,32,512]{2,1,0:T(8,128)(2,1)}) %reduce-scatter.11.cloned.1.call-update) | async-done | bytes 524304 | tf_op jit(solution)/shard_map/reduce_scatter | solution.py:606
  425.3 14.7 %fourth.1 = (bf16[8,192,512]{2,1,0:T(8,128)(2,1)}, f32[16,192,256]{2,1,0:T(8,128)}, f32[192,1024]{1,0:T(8,128)}) custom-call(bf16[4,62,32,512]{3,2,1,0:T(8,128)(2,1)} %all-gather.6.cloned.1.call-done.w_hbm, bf16[16,192,512]{2,1,0:T(8,128)(2,1)} %get-tuple-element.27.skip_ref, bf16[16,192,512]{2,1,0:T(8,128)(2,1)} %get-tuple-element.32.g1_ref, ...), custom_call_target="tpu_custom_call" | custom-call | tf_op jit(solution)/shard_map/fourth/pallas_call | solution.py:518
  440.0 5.5 %copy.40 = f32[4,48,16,256]{3,2,1,0:T(8,128)} copy(f32[4,48,16,256]{3,1,0,2:T(8,128)} %bitcast.36) | data formatting | bytes 6291456
  445.6 2.0 copy.39
  447.6 3.4 copy.38
  451.1 40.4 %psum.7 = f32[10,512]{1,0:T(8,128)S(1)} all-reduce(f32[10,512]{1,0:T(8,128)S(1)} %pad_maximum_fusion.3), channel_id=1, replica_groups=mesh['dp'=8,'pair'=4] {'dp','pair'}, use_global_device_ids=true, to_apply=%region_6.7 | all-reduce | flops 5120 | bytes 40960 | tf_op jit(solution)/shard_map/psum | solution.py:602
  492.2 10.0 %multiply_subtract_fusion = (f32[16,128,512]{2,1,0:T(8,128)}, f32[16,128,512]{2,1,0:T(8,128)}, f32[16,128,512]{2,1,0:T(8,128)}) fusion(f32[16,128,512]{2,1,0:T(8,128)} %param.20, bf16[16,128,512]{2,1,0:T(8,128)(2,1)} %all-gather.8.cloned.1.call-done, pred[16]{0:T(512)(128)(4,1)S(1)} %dynamic-slice_compare_fusion, f32[16,128,512]{2,1,0:T(8,128)} %param.22, ...), kind=kLoop, calls=%fused_computation.5 | loop fusion | flops 17825792 | bytes 27262992 | tf_op jit(solution)/shard_map/sub | solution.py:70
  (57 shorter events, 3.9 us)
Async XLA Ops:
  7.2 79.7 %all-gather.4.cloned.1.call-start = ((), (), s32[]{:S(2)}) async-start(), calls=%async_computation.4 | async-start | bytes 4718592 | tf_op jit(solution)/shard_map/all_gather | solution.py:591
  9.4 139.3 %all-gather.6.cloned.1.call-start = ((), (), s32[]{:S(2)}) async-start(), calls=%async_computation.5 | async-start | bytes 10158080 | tf_op jit(solution)/shard_map/all_gather | solution.py:593
  11.0 80.4 %copy-start.9 = (s32[4,48]{1,0:T(4,128)S(1)}, s32[4,48]{1,0:T(4,128)}, u32[]{:S(2)}) copy-start(s32[4,48]{1,0:T(4,128)} %param.16) | copy-start | bytes 2308
  89.7 3.8 copy-start.10
  91.3 187.8 %reduce-scatter.7.cloned.1.call-start = ((), (), s32[]{:S(2)}) async-start(), calls=%async_computation.7 | async-start | bytes 4587520 | tf_op jit(solution)/shard_map/reduce_scatter | solution.py:601
  91.5 7.5 %copy-start.1 = (bf16[4,48,8,512]{3,2,1,0:T(8,128)(2,1)S(1)}, bf16[4,48,8,512]{3,2,1,0:T(8,128)(2,1)}, u32[]{:S(2)}) copy-start(bf16[4,48,8,512]{3,2,1,0:T(8,128)(2,1)} %param.18) | copy-start | bytes 4718596
  93.6 7.6 %copy-start.4 = (bf16[4,48,256]{2,1,0:T(8,128)(2,1)S(1)}, bf16[4,48,256]{2,1,0:T(8,128)(2,1)}, u32[]{:S(2)}) copy-start(bf16[4,48,256]{2,1,0:T(8,128)(2,1)} %param.14) | copy-start | bytes 294916
  237.8 90.2 %reduce-scatter.9.cloned.1.call-start = ((), (), s32[]{:S(2)}) async-start(), calls=%async_computation.8 | async-start | bytes 5570560 | tf_op jit(solution)/shard_map/reduce_scatter | solution.py:600
  238.3 186.8 %reduce-scatter.11.cloned.1.call-start = ((), (), s32[]{:S(2)}) async-start(), calls=%async_computation.9 | async-start | bytes 4718592 | tf_op jit(solution)/shard_map/reduce_scatter | solution.py:606
  336.9 155.3 %all-gather.8.cloned.1.call-start = ((), (), s32[]{:S(2)}) async-start(), calls=%async_computation.10 | async-start | bytes 2621440 | tf_op jit(solution)/shard_map/all_gather | solution.py:607
  425.1 77.0 %reduce-scatter.5.cloned.1.call-start = ((), (), s32[]{:S(2)}) async-start(), calls=%async_computation.6 | async-start | bytes 983040 | tf_op jit(solution)/shard_map/reduce_scatter | solution.py:603
  425.3 14.7 %copy-start.7 = (f32[8,512]{1,0:T(8,128)S(1)}, f32[8,512]{1,0:T(8,128)}, u32[]{:S(2)}) copy-start(f32[8,512]{1,0:T(8,128)} %get-tuple-element.41) | copy-start | bytes 49156
  425.3 14.7 %copy-start.8 = (f32[8,512]{1,0:T(8,128)S(1)}, f32[8,512]{1,0:T(8,128)}, u32[]{:S(2)}) copy-start(f32[8,512]{1,0:T(8,128)} %get-tuple-element.40) | copy-start | bytes 49156
  440.0 5.6 %copy-start.2 = (bf16[8,192,512]{2,1,0:T(8,128)(2,1)S(1)}, bf16[8,192,512]{2,1,0:T(8,128)(2,1)}, u32[]{:S(2)}) copy-start(bf16[8,192,512]{2,1,0:T(8,128)(2,1)} %get-tuple-element.35) | copy-start | bytes 4718596
  440.0 7.6 %copy-start = (bf16[16,192,512]{2,1,0:T(8,128)(2,1)S(1)}, bf16[16,192,512]{2,1,0:T(8,128)(2,1)}, u32[]{:S(2)}) copy-start(bf16[16,192,512]{2,1,0:T(8,128)(2,1)} %get-tuple-element.27.skip_ref) | copy-start | bytes 9437188
  445.6 45.9 %copy-start.3 = (f32[10,512]{1,0:T(8,128)S(1)}, f32[10,512]{1,0:T(8,128)}, u32[]{:S(2)}) copy-start(f32[10,512]{1,0:T(8,128)} %small_ref.7) | copy-start | bytes 61444
  445.6 45.9 %copy-start.5 = (f32[10,512]{1,0:T(8,128)S(1)}, f32[10,512]{1,0:T(8,128)}, u32[]{:S(2)}) copy-start(f32[10,512]{1,0:T(8,128)} %param.25) | copy-start | bytes 61444
  445.6 45.9 %copy-start.6 = (f32[10,512]{1,0:T(8,128)S(1)}, f32[10,512]{1,0:T(8,128)}, u32[]{:S(2)}) copy-start(f32[10,512]{1,0:T(8,128)} %param.24) | copy-start | bytes 61444
Sparse Core Ops, SparseCore 0:
  10.7 76.0 all-gather.3
  91.4 57.1 all-gather.5
  237.9 41.2 reduce-scatter.6
  281.7 46.1 reduce-scatter.8
  337.0 88.0 reduce-scatter.10
  426.6 22.3 all-gather.7
  452.3 23.2 reduce-scatter.4

commit v2 on v1

v2 whole, which is shorter than its diff:
```python
import functools
import math

import jax
import jax.numpy as jnp
from jax import lax
from jax.experimental import pallas as pl
from jax.experimental.pallas import tpu as pltpu
from jax.sharding import PartitionSpec as P

CI = 256
C = 512
TE = 128
KW = 5
H = 16
HD = 8
KD = 3
NSMALL = 10
STEP = 10
BLK = 128
COND = 1152
NBLK = 62
GC = 64

FIRST_N, SECOND_N, RES_N, DOWN_N, FILM_N = 10, 20, 2, 12, 9
EARLY_N = FIRST_N + 2 * FILM_N
LATE_N = SECOND_N + RES_N + DOWN_N
DOWN_IN = SECOND_N + RES_N
PIECES = 32

BETA_ONE = 0.9
BETA_TWO = 0.999
EPS_ADAM = 1e-08
DECAY = 0.01
RATE_MATRIX = 0.1
RATE_SMALL = 1.0

F32 = jnp.float32
BF = jnp.bfloat16
NT = (((1,), (1,)), ((), ()))
TN = (((0,), (0,)), ((), ()))
VMEM_LIMIT = 56 * 2**20


def mish(value):
    return value * jnp.tanh(jax.nn.softplus(value))


def time_embed(step_ids, width):
    half = width // 2
    freq = jnp.exp(-math.log(10000.0) * jnp.arange(half, dtype=F32) / (half - 1))
    angle = step_ids.astype(F32)[:, None] * freq[None, :]
    return jnp.concatenate([jnp.sin(angle), jnp.cos(angle)], axis=1)


def slot_of(owners, slot_count):
    same = owners[:, None] == owners[None, :]
    order = jnp.arange(owners.shape[0], dtype=jnp.int32)
    earlier = order[:, None] > order[None, :]
    rank = jnp.sum((same & earlier).astype(jnp.int32), axis=1)
    return owners * slot_count + rank


def adamw(weight, first_m, second_m, grad, rate):
    first_new = BETA_ONE * first_m + (1.0 - BETA_ONE) * grad
    second_new = BETA_TWO * second_m + (1.0 - BETA_TWO) * grad * grad
    fix_one = 1.0 - BETA_ONE**STEP
    fix_two = 1.0 - BETA_TWO**STEP
    update = first_new / fix_one / (jnp.sqrt(second_new / fix_two) + EPS_ADAM) + DECAY * weight
    return (first_new, second_new, weight - rate * update)


def recip(value):
    r = pl.reciprocal(value, approx=True)
    return r * (2.0 - value * r)


def mish_parts(v):
    w = jnp.exp(jnp.minimum(v, 30.0))
    n = w * (w + 2.0)
    r = recip(n + 2.0)
    return w, n * r, r


def mish_only(v):
    _, t, _ = mish_parts(v)
    return v * t


def mish_both(v):
    w, t, r = mish_parts(v)
    return v * t, t + (4.0 * v) * (((w * (1.0 + w)) * r) * r)


def group_sum(value):
    low_half = lax.broadcasted_iota(jnp.int32, value.shape, 1) < GC
    zero = jnp.zeros_like(value)
    left = jnp.sum(jnp.where(low_half, value, zero), axis=1, keepdims=True)
    right = jnp.sum(jnp.where(low_half, zero, value), axis=1, keepdims=True)
    return jnp.where(low_half, left, right)


def lanes(q):
    return slice(q * 128, (q + 1) * 128)


def flips_of(k):
    return (k >> 3) & 1, (k >> 2) & 1, (k >> 1) & 1, k & 1


def place(me, k, by_y_first, core):
    one, two, z_low, z_high = flips_of(k)
    y, x = (one, two) if by_y_first else (two, one)
    return me[0] ^ (z_high * 4 + z_low * 2 + y), me[1] ^ (x * 2 + core)


def fetch(me, sources, dst, sem):
    at = 0
    for by_y_first, pair in ((False, sources[:2]), (True, sources[2:])):
        count = pair[0].shape[1]
        for core, source in enumerate(pair):
            for k in range(16):
                row, col = place(me, k, by_y_first, core)
                pltpu.make_async_copy(
                    source.at[k],
                    dst.at[at : at + count, row, :, pl.ds(pl.multiple_of(col * 128, 128), 128)],
                    sem,
                ).start()
        at = at + count
    return pltpu.make_async_copy(dst, dst, sem)


def store_pieces(me, acc, outs, base=0):
    at = 0
    for by_y_first, pair in ((False, outs[:2]), (True, outs[2:])):
        count = pair[0].shape[1]

        def one_block(b, carry, at=at, by_y_first=by_y_first, pair=pair):
            for core, out in enumerate(pair):
                for k in range(16):
                    row, col = place(me, k, by_y_first, core)
                    rows = pl.ds(pl.multiple_of((at + b) * BLK + row * 16, 16), 16)
                    cols = pl.ds(pl.multiple_of(col * 128, 128), 128)
                    out[k, b] = acc[rows, cols].astype(BF)
            return carry

        lax.fori_loop(0, count, one_block, 0)
        at = at + count


def matrix(ref, at, count):
    return ref[at : at + count].reshape(count * BLK, C)


def first_kernel(me, pa, pb, pc, pd, x_ref, cond_ref, lens_ref, inv_ref, small_ref, normed_ref, rstd_ref, hid_ref,
                 mod_ref, w_out, w_one, xp, fst, sem):
    step = pl.program_id(0)
    frames, width, _ = x_ref.shape
    rows = frames * width

    @pl.when(step == 0)
    def _():
        arrival = fetch((me[0], me[1]), (pa, pb, pc, pd), w_one, sem.at[0])
        xp[0:2] = jnp.zeros((2, width, CI), BF)
        xp[frames + 2 :] = jnp.zeros((2, width, CI), BF)
        arrival.wait()
        pltpu.make_async_copy(w_one, w_out, sem.at[1]).start()
        for k in range(2):
            mod_ref[k] = (
                jnp.dot(cond_ref[...], matrix(w_one, FIRST_N + k * FILM_N, FILM_N), preferred_element_type=F32)
                + small_ref[3 + k : 4 + k]
            )

    xp[2 : frames + 2] = x_ref[...]
    acc = jnp.dot(xp[0:frames].reshape(rows, CI), matrix(w_one, 0, 2), preferred_element_type=F32)
    for a in range(1, KW):
        acc = acc + jnp.dot(
            xp[a : a + frames].reshape(rows, CI), matrix(w_one, 2 * a, 2), preferred_element_type=F32
        )
    fst[...] = (acc + small_ref[0:1]).reshape(frames, width, C)

    here = pl.ds(pl.multiple_of(step * width, width), width)
    lens = lens_ref[...]
    inv = inv_ref[...]
    for q in range(C // 128):
        ls = lanes(q)
        total = jnp.zeros((width, 128), F32)
        for t in range(frames):
            total = total + jnp.where(lens > t, fst[t, :, ls], 0.0)
        mean = group_sum(total) * inv
        total = jnp.zeros((width, 128), F32)
        for t in range(frames):
            centered = fst[t, :, ls] - mean
            total = total + jnp.where(lens > t, centered * centered, 0.0)
        rstd = lax.rsqrt(group_sum(total) * inv + 1e-05)
        rstd_ref[:, ls] = rstd
        gain, bias = small_ref[1:2, ls], small_ref[2:3, ls]
        scale, shift = mod_ref[0, here, ls], mod_ref[1, here, ls]
        for t in range(frames):
            normed = (fst[t, :, ls] - mean) * rstd
            normed_ref[t, :, ls] = normed
            value = scale * mish_only(normed * gain + bias) + shift
            hid_ref[t, :, ls] = jnp.where(lens > t, value, 0.0).astype(BF)

    @pl.when(step == pl.num_programs(0) - 1)
    def _():
        pltpu.make_async_copy(w_one, w_out, sem.at[1]).wait()


def second_kernel(me, pa, pb, pc, pd, hid_ref, x_ref, cs_ref, cd_ref, lens_ref, inv_ref, small_ref, skip_ref,
                  dskip_ref, g2_ref, ga, gb, gc, gd, gs_ref, w_out, w_two, hp, cdp, sec, br, dev, dod, se, so, acc,
                  sem):
    step = pl.program_id(0)
    last = pl.num_programs(0) - 1
    frames, width, _ = x_ref.shape
    half = frames // 2
    rows = frames * width

    @pl.when(step == 0)
    def _():
        arrival = fetch((me[0], me[1]), (pa, pb, pc, pd), w_two, sem.at[0])
        hp[0:2] = jnp.zeros((2, width, C), BF)
        hp[frames + 2 :] = jnp.zeros((2, width, C), BF)
        cdp[half:] = jnp.zeros((1, width, C), BF)
        so[0:1] = jnp.zeros((1, width, C), BF)
        acc[...] = jnp.zeros_like(acc)
        gs_ref[...] = jnp.zeros_like(gs_ref)
        arrival.wait()
        pltpu.make_async_copy(w_two, w_out, sem.at[1]).start()

    hp[2 : frames + 2] = hid_ref[...]
    cdp[0:half] = cd_ref[...]
    cot = cdp[0:half].reshape(half * width, C)
    cot_next = cdp[1 : half + 1].reshape(half * width, C)
    dev[...] = lax.dot_general(cot, matrix(w_two, DOWN_IN + 4, 4), NT, preferred_element_type=F32).reshape(half, width, C)
    dod[...] = (
        lax.dot_general(cot, matrix(w_two, DOWN_IN + 8, 4), NT, preferred_element_type=F32)
        + lax.dot_general(cot_next, matrix(w_two, DOWN_IN + 0, 4), NT, preferred_element_type=F32)
    ).reshape(half, width, C)
    br[...] = (
        jnp.dot(x_ref[...].reshape(rows, CI), matrix(w_two, SECOND_N, RES_N), preferred_element_type=F32) + small_ref[8:9]
    ).reshape(frames, width, C)
    total = jnp.dot(hp[0:frames].reshape(rows, C), matrix(w_two, 0, 4), preferred_element_type=F32)
    for a in range(1, KW):
        total = total + jnp.dot(
            hp[a : a + frames].reshape(rows, C), matrix(w_two, 4 * a, 4), preferred_element_type=F32
        )
    sec[...] = (total + small_ref[5:6]).reshape(frames, width, C)

    lens = lens_ref[...]
    inv = inv_ref[...]
    zero = jnp.zeros((width, 128), F32)
    for q in range(C // 128):
        ls = lanes(q)
        total = zero
        for t in range(frames):
            total = total + jnp.where(lens > t, sec[t, :, ls], 0.0)
        mean = group_sum(total) * inv
        total = zero
        for t in range(frames):
            centered = sec[t, :, ls] - mean
            total = total + jnp.where(lens > t, centered * centered, 0.0)
        rstd = lax.rsqrt(group_sum(total) * inv + 1e-05)
        gain, bias = small_ref[6:7, ls], small_ref[7:8, ls]
        sum_dy, sum_dyn, sum_ds = zero, zero, zero
        for t in range(frames):
            normed = (sec[t, :, ls] - mean) * rstd
            sec[t, :, ls] = normed
            act, slope = mish_both(normed * gain + bias)
            skip = (act + br[t, :, ls]).astype(BF)
            skip_ref[t, :, ls] = skip
            if t % 2:
                so[t // 2 + 1, :, ls] = skip
                back = dod[t // 2, :, ls]
            else:
                se[t // 2, :, ls] = skip
                back = dev[t // 2, :, ls]
            ds = (cs_ref[t, :, ls].astype(F32) + back).astype(BF)
            dskip_ref[t, :, ls] = ds
            ds = ds.astype(F32)
            sum_ds = sum_ds + ds
            dy = ds * slope
            br[t, :, ls] = dy
            sum_dy = sum_dy + dy
            sum_dyn = sum_dyn + dy * normed
        mean_a = group_sum(sum_dy * gain) * inv
        mean_an = group_sum(sum_dyn * gain) * inv
        sum_g, sum_cd = zero, zero
        for t in range(frames):
            normed = sec[t, :, ls]
            grad = rstd * (br[t, :, ls] * gain - jnp.where(lens > t, mean_a + normed * mean_an, 0.0))
            grad = grad.astype(BF)
            g2_ref[t, :, ls] = grad
            sum_g = sum_g + grad.astype(F32)
        for t in range(half):
            sum_cd = sum_cd + cd_ref[t, :, ls].astype(F32)
        for k, part in enumerate((sum_g, sum_dyn, sum_dy, sum_ds, sum_cd)):
            gs_ref[k : k + 1, ls] += jnp.sum(part, axis=0, keepdims=True)

    grad_two = g2_ref[...].reshape(rows, C)
    for a in range(KW):
        acc[a * C : (a + 1) * C] += lax.dot_general(
            hp[a : a + frames].reshape(rows, C), grad_two, TN, preferred_element_type=F32
        )
    at = KW * C
    acc[at : at + CI] += lax.dot_general(
        x_ref[...].reshape(rows, CI), dskip_ref[...].reshape(rows, C), TN, preferred_element_type=F32
    )
    at = at + CI
    for a, source in enumerate((so.at[0:half], se, so.at[1 : half + 1])):
        acc[at + a * C : at + (a + 1) * C] += lax.dot_general(
            source[...].reshape(half * width, C), cot, TN, preferred_element_type=F32
        )

    @pl.when(step == last)
    def _():
        store_pieces((me[0], me[1]), acc, (ga, gb, gc, gd))
        pltpu.make_async_copy(w_two, w_out, sem.at[1]).wait()


def third_kernel(me, w_hbm, g2_ref, x_ref, cond_ref, normed_ref, rstd_ref, mod_ref, lens_ref, inv_ref, small_ref,
                 g1_ref, dmod_ref, ga, gb, gc, gd, gs_ref, w_two, gp, xp, dh, acc, sem):
    step = pl.program_id(0)
    last = pl.num_programs(0) - 1
    frames, width, _ = x_ref.shape
    rows = frames * width

    @pl.when(step == 0)
    def _():
        arrival = pltpu.make_async_copy(w_hbm.at[0:SECOND_N], w_two, sem.at[0])
        arrival.start()
        gp[0:2] = jnp.zeros((2, width, C), BF)
        gp[frames + 2 :] = jnp.zeros((2, width, C), BF)
        xp[0:2] = jnp.zeros((2, width, CI), BF)
        xp[frames + 2 :] = jnp.zeros((2, width, CI), BF)
        acc[...] = jnp.zeros_like(acc)
        gs_ref[...] = jnp.zeros_like(gs_ref)
        arrival.wait()

    gp[2 : frames + 2] = g2_ref[...]
    xp[2 : frames + 2] = x_ref[...]
    total = lax.dot_general(gp[4 : 4 + frames].reshape(rows, C), matrix(w_two, 0, 4), NT, preferred_element_type=F32)
    for a in range(1, KW):
        total = total + lax.dot_general(
            gp[4 - a : 4 - a + frames].reshape(rows, C), matrix(w_two, 4 * a, 4), NT, preferred_element_type=F32
        )
    dh[...] = total.reshape(frames, width, C)

    here = pl.ds(pl.multiple_of(step * width, width), width)
    lens = lens_ref[...]
    inv = inv_ref[...]
    zero = jnp.zeros((width, 128), F32)
    for q in range(C // 128):
        ls = lanes(q)
        gain, bias = small_ref[1:2, ls], small_ref[2:3, ls]
        scale = mod_ref[0, here, ls]
        sum_dy, sum_dyn, d_scale, d_shift = zero, zero, zero, zero
        for t in range(frames):
            normed = normed_ref[t, :, ls]
            act, slope = mish_both(normed * gain + bias)
            grad = jnp.where(lens > t, dh[t, :, ls], 0.0)
            d_scale = d_scale + grad * act
            d_shift = d_shift + grad
            dy = (grad * scale) * slope
            dh[t, :, ls] = dy
            sum_dy = sum_dy + dy
            sum_dyn = sum_dyn + dy * normed
        mean_a = group_sum(sum_dy * gain) * inv
        mean_an = group_sum(sum_dyn * gain) * inv
        rstd = rstd_ref[:, ls]
        sum_g = zero
        for t in range(frames):
            normed = normed_ref[t, :, ls]
            grad = rstd * (dh[t, :, ls] * gain - jnp.where(lens > t, mean_a + normed * mean_an, 0.0))
            grad = grad.astype(BF)
            g1_ref[t, :, ls] = grad
            sum_g = sum_g + grad.astype(F32)
        d_scale, d_shift = d_scale.astype(BF), d_shift.astype(BF)
        dmod_ref[0, here, ls] = d_scale
        dmod_ref[1, here, ls] = d_shift
        for k, part in enumerate((sum_g, sum_dyn, sum_dy, d_scale.astype(F32), d_shift.astype(F32))):
            gs_ref[k : k + 1, ls] += jnp.sum(part, axis=0, keepdims=True)

    grad_one = g1_ref[...].reshape(rows, C)
    for a in range(KW):
        acc[a * CI : (a + 1) * CI] += lax.dot_general(
            xp[a : a + frames].reshape(rows, CI), grad_one, TN, preferred_element_type=F32
        )

    @pl.when(step == last)
    def _():
        for k in range(2):
            at = KW * CI + k * COND
            acc[at : at + COND] = lax.dot_general(cond_ref[...], dmod_ref[k], TN, preferred_element_type=F32)
        store_pieces((me[0], me[1]), acc, (ga, gb, gc, gd))


def fourth_kernel(w_early, w_late, skip_ref, g1_ref, dskip_ref, dmod_ref, slope_ref, lens_ref, small_ref, down_ref, dx_ref,
                  dobs_ref, w_one, w_two, gp, se, so, sem):
    step = pl.program_id(0)
    frames, width, _ = skip_ref.shape
    half = frames // 2
    rows = frames * width

    @pl.when(step == 0)
    def _():
        early = pltpu.make_async_copy(w_early, w_one, sem.at[0])
        late = pltpu.make_async_copy(w_late.at[SECOND_N:LATE_N], w_two, sem.at[1])
        early.start()
        late.start()
        gp[0:2] = jnp.zeros((2, width, C), BF)
        gp[frames + 2 :] = jnp.zeros((2, width, C), BF)
        so[0:1] = jnp.zeros((1, width, C), BF)
        early.wait()
        back = lax.dot_general(dmod_ref[0], matrix(w_one, FIRST_N + 1, FILM_N - 1), NT, preferred_element_type=F32)
        back = back + lax.dot_general(
            dmod_ref[1], matrix(w_one, FIRST_N + FILM_N + 1, FILM_N - 1), NT, preferred_element_type=F32
        )
        dobs_ref[...] = back * slope_ref[...]
        late.wait()

    gp[2 : frames + 2] = g1_ref[...]
    total = lax.dot_general(dskip_ref[...].reshape(rows, C), matrix(w_two, 0, RES_N), NT, preferred_element_type=F32)
    for a in range(KW):
        total = total + lax.dot_general(
            gp[4 - a : 4 - a + frames].reshape(rows, C), matrix(w_one, 2 * a, 2), NT, preferred_element_type=F32
        )
    total = total.reshape(frames, width, CI)
    lens = lens_ref[...]
    for t in range(frames):
        for q in range(CI // 128):
            dx_ref[t, :, lanes(q)] = jnp.where(lens > t, total[t, :, lanes(q)], 0.0)
    for j in range(half):
        se[j] = skip_ref[2 * j]
        so[j + 1] = skip_ref[2 * j + 1]
    down = jnp.dot(so[0:half].reshape(half * width, C), matrix(w_two, RES_N + 0, 4), preferred_element_type=F32)
    down = down + jnp.dot(se[...].reshape(half * width, C), matrix(w_two, RES_N + 4, 4), preferred_element_type=F32)
    down = down + jnp.dot(
        so[1 : half + 1].reshape(half * width, C), matrix(w_two, RES_N + 8, 4), preferred_element_type=F32
    )
    down_ref[...] = (down + small_ref[9:10]).astype(BF).reshape(half, width, C)


def adamw_kernel(me, used, own_ref, recv_ref, master_ref, one_ref, two_ref, one_out, two_out, master_out, grad):
    for slot in range(grad.shape[0]):
        keep = used[pl.program_id(0) * grad.shape[0] + slot] > 0
        for core, source in enumerate((own_ref, recv_ref)):
            for x in range(2):
                cols = pl.ds(pl.multiple_of((me[1] ^ (x * 2 + core)) * 128, 128), 128)
                for row in range(8):
                    piece = source[x, row, slot].astype(F32)
                    grad[slot, row * 16 : row * 16 + 16, cols] = jnp.where(keep, piece, 0.0)
    one_out[...], two_out[...], master_out[...] = adamw(
        master_ref[...], one_ref[...], two_ref[...], grad[...], RATE_MATRIX
    )


def tiles(frames, width, channels):
    return pl.BlockSpec((frames, width, channels), lambda i, *_: (0, i, 0))


def rows_of(width, channels):
    return pl.BlockSpec((width, channels), lambda i, *_: (i, 0))


def whole(*shape):
    return pl.BlockSpec(shape, lambda i, *_: (0,) * len(shape))


ANY = pl.BlockSpec(memory_space=pl.ANY)
PARAMS = pltpu.CompilerParams(vmem_limit_bytes=VMEM_LIMIT, dimension_semantics=("arbitrary",))


def weight_scratch(count):
    return pltpu.VMEM((count, 8, 16, C), BF)


def shape(*dims, dtype=F32):
    return jax.ShapeDtypeStruct(dims, dtype)


def half_lists(count):
    front = count // 2
    return [(16, n, 16, 128) for n in (front, front, count - front, count - front)]


def call(kernel, name, grid, scalars, ins, outs, scratch, operands, flops):
    return pl.pallas_call(
        kernel,
        grid_spec=pltpu.PrefetchScalarGridSpec(
            num_scalar_prefetch=scalars,
            grid=grid,
            in_specs=ins,
            out_specs=[spec for spec, _ in outs],
            scratch_shapes=scratch,
        ),
        out_shape=[made for _, made in outs],
        compiler_params=PARAMS,
        cost_estimate=pl.CostEstimate(flops=flops, bytes_accessed=20 * 2**20, transcendentals=0),
        name=name,
    )(*operands)


def run_first(me, pieces, x, cond, lens, inv, small, width):
    count = x.shape[1]
    return call(
        first_kernel, "first", (count // width,), 1,
        [ANY] * 4 + [tiles(H, width, CI), whole(count, COND), rows_of(width, 128), rows_of(width, 128),
                     whole(NSMALL, C)],
        [(tiles(H, width, C), shape(H, count, C)), (rows_of(width, C), shape(count, C)),
         (tiles(H, width, C), shape(H, count, C, dtype=BF)), (whole(2, count, C), shape(2, count, C)),
         (ANY, shape(EARLY_N, 8, 16, C, dtype=BF))],
        [weight_scratch(EARLY_N), pltpu.VMEM((H + 4, width, CI), BF), pltpu.VMEM((H, width, C), F32),
         pltpu.SemaphoreType.DMA((2,))],
        (me, *pieces, x, cond, lens, inv, small),
        2 * count * H * KW * CI * C,
    )


def run_second(me, pieces, hid, x, cs, cd, lens, inv, small, width):
    count = x.shape[1]
    bf_tile = (tiles(H, width, C), shape(H, count, C, dtype=BF))
    return call(
        second_kernel, "second", (count // width,), 1,
        [ANY] * 4 + [tiles(H, width, C), tiles(H, width, CI), tiles(H, width, C), tiles(HD, width, C),
                     rows_of(width, 128), rows_of(width, 128), whole(NSMALL, C)],
        [bf_tile, bf_tile, bf_tile] + [(whole(*dims), shape(*dims, dtype=BF)) for dims in half_lists(LATE_N)]
        + [(whole(8, C), shape(8, C)), (ANY, shape(LATE_N, 8, 16, C, dtype=BF))],
        [weight_scratch(LATE_N), pltpu.VMEM((H + 4, width, C), BF), pltpu.VMEM((HD + 1, width, C), BF),
         pltpu.VMEM((H, width, C), F32), pltpu.VMEM((H, width, C), F32),
         pltpu.VMEM((HD, width, C), F32), pltpu.VMEM((HD, width, C), F32),
         pltpu.VMEM((HD, width, C), BF), pltpu.VMEM((HD + 1, width, C), BF),
         pltpu.VMEM((LATE_N * BLK, C), F32), pltpu.SemaphoreType.DMA((2,))],
        (me, *pieces, hid, x, cs, cd, lens, inv, small),
        6 * count * H * KW * C * C,
    )


def run_third(me, w_late, g2, x, cond, normed, rstd, mod, lens, inv, small, width):
    count = x.shape[1]
    return call(
        third_kernel, "third", (count // width,), 1,
        [ANY, tiles(H, width, C), tiles(H, width, CI), whole(count, COND), tiles(H, width, C),
         rows_of(width, C), whole(2, count, C), rows_of(width, 128), rows_of(width, 128), whole(NSMALL, C)],
        [(tiles(H, width, C), shape(H, count, C, dtype=BF)), (whole(2, count, C), shape(2, count, C, dtype=BF))]
        + [(whole(*dims), shape(*dims, dtype=BF)) for dims in half_lists(EARLY_N)] + [(whole(8, C), shape(8, C))],
        [weight_scratch(SECOND_N), pltpu.VMEM((H + 4, width, C), BF),
         pltpu.VMEM((H + 4, width, CI), BF), pltpu.VMEM((H, width, C), F32),
         pltpu.VMEM((EARLY_N * BLK, C), F32), pltpu.SemaphoreType.DMA((1,))],
        (me, w_late, g2, x, cond, normed, rstd, mod, lens, inv, small),
        4 * count * H * KW * C * C,
    )


def run_fourth(w_early, w_late, skip, g1, dskip, dmod, slope, lens, small, width):
    count = skip.shape[1]
    features = slope.shape[1]
    return call(
        fourth_kernel, "fourth", (count // width,), 0,
        [ANY, ANY, tiles(H, width, C), tiles(H, width, C), tiles(H, width, C), whole(2, count, C),
         whole(count, features), rows_of(width, 128), whole(NSMALL, C)],
        [(tiles(HD, width, C), shape(HD, count, C, dtype=BF)), (tiles(H, width, CI), shape(H, count, CI)),
         (whole(count, features), shape(count, features))],
        [weight_scratch(EARLY_N), weight_scratch(RES_N + DOWN_N), pltpu.VMEM((H + 4, width, C), BF),
         pltpu.VMEM((HD, width, C), BF), pltpu.VMEM((HD + 1, width, C), BF), pltpu.SemaphoreType.DMA((2,))],
        (w_early, w_late, skip, g1, dskip, dmod, slope, lens, small),
        2 * count * H * KW * C * C,
    )


def run_adamw(me, used, own, recv, master, one, two):
    slots = master.shape[0]
    group = 2
    block = pl.BlockSpec((group, BLK, C), lambda i, *_: (i, 0, 0))
    piece = pl.BlockSpec((2, 8, group, 16, 128), lambda i, *_: (0, 0, i, 0, 0))
    return call(
        adamw_kernel, "adamw", (slots // group,), 2,
        [piece, piece, block, block, block],
        [(block, shape(slots, BLK, C))] * 3,
        [pltpu.VMEM((group, BLK, C), F32)],
        (me, used, own, recv, master, one, two),
        20 * slots * BLK * C,
    )


def prepare(actions, shared, tsteps, lengths, cot_skip, cot_down):
    micro, samp = lengths.shape
    count = micro * samp
    lens_flat = lengths.reshape(count)
    lens = jnp.broadcast_to(lens_flat.astype(F32)[:, None], (count, 128))
    inv = 1.0 / (lens * GC)
    keep = jnp.arange(H)[:, None, None] < lens_flat[None, :, None]
    x = jnp.where(keep, actions.reshape(count, H, CI).transpose(1, 0, 2), jnp.zeros((), BF))
    cs = cot_skip.reshape(count, H, C).transpose(1, 0, 2)
    cd = cot_down.reshape(count, HD, C).transpose(1, 0, 2)
    obs = shared.reshape(count, -1).astype(F32)
    obs_act, obs_back = jax.vjp(mish, obs)
    slope = obs_back(jnp.ones_like(obs))[0]
    cond = jnp.concatenate([mish(time_embed(tsteps.reshape(count), TE)), obs_act], axis=1).astype(BF)
    return x, cs, cd, lens, inv, cond, slope


def flip(value, axis, bit):
    size = lax.axis_size(axis)
    return lax.ppermute(value, axis, [(i, i ^ bit) for i in range(size)])


def core(value):
    return flip(value, "pair", 1)


def along_x(value):
    return flip(value, "pair", 2)


def along_y(value):
    return flip(value, "dp", 1)


def z_low(value):
    return flip(value, "dp", 2)


def z_high(value):
    return flip(value, "dp", 4)


def pieces_of(block):
    return block.reshape(-1, 8, 16, 4, 128).transpose(1, 3, 0, 2, 4)


def double(value, hop):
    return jnp.concatenate([value, hop(value)], axis=0)


def gather_list(mine):
    value = double(double(mine[None], z_high), z_low)
    front = mine.shape[0] // 2
    a, b = value[:, :front], value[:, front:]
    a = double(double(a, along_y), along_x)
    b = double(double(b, along_x), along_y)
    return a, core(a), b, core(b)


def halve(value, hop):
    size = value.shape[0] // 2
    return value[:size] + hop(value[size:])


def reduce_list(lists):
    a_own, a_other, b_own, b_other = lists
    a = a_own + core(a_other)
    b = b_own + core(b_other)
    a = halve(halve(a, along_x), along_y)
    b = halve(halve(b, along_y), along_x)
    value = jnp.concatenate([a, b], axis=1)
    return halve(halve(value, z_low), z_high)[0]


def sum_all(value):
    for axis in ("pair", "dp"):
        bit = 1
        while bit < lax.axis_size(axis):
            value = value + flip(value, axis, bit)
            bit = bit * 2
    return value


def split_order(blocks):
    return jnp.concatenate([blocks[:FIRST_N], blocks[FIRST_N + LATE_N :]], axis=0), blocks[FIRST_N : FIRST_N + LATE_N]


def join_order(early, late):
    return jnp.concatenate([early[:FIRST_N], late, early[FIRST_N:]], axis=0)


def as_lists(blocks):
    front = blocks.shape[0] // 2
    found = []
    for by_y_first, part in ((False, blocks[:front]), (True, blocks[front:])):
        cut = pieces_of(part)
        for core_bit in range(2):
            found.append(jnp.stack([cut[place((0, 0), k, by_y_first, core_bit)] for k in range(16)]))
    return tuple(found)


def from_lists(lists):
    parts = []
    for by_y_first, pair in ((False, lists[:2]), (True, lists[2:])):
        table = {}
        for core_bit, part in enumerate(pair):
            for k in range(16):
                table[place((0, 0), k, by_y_first, core_bit)] = part[k]
        cut = jnp.stack([jnp.stack([table[(row, col)] for col in range(4)]) for row in range(8)])
        parts.append(cut.transpose(2, 0, 3, 1, 4).reshape(-1, BLK, C))
    return jnp.concatenate(parts, axis=0)


def body(
    actions,
    observations,
    tsteps,
    lengths,
    cot_skip,
    cot_down,
    owners,
    master,
    moment_one,
    moment_two,
    small_master,
    small_one,
    small_two,
):
    micro, samp = lengths.shape
    slot_count = master.shape[0]
    dp_count = lax.axis_size("dp")
    slots_all = dp_count * slot_count
    me_pair = lax.axis_index("pair")
    me_dp = lax.axis_index("dp")
    by_pieces = dp_count == 8 and lax.axis_size("pair") == 4
    slot_index = slot_of(owners, slot_count)
    block_of = (
        jnp.full((slots_all,), -1, jnp.int32).at[slot_index].set(jnp.arange(NBLK, dtype=jnp.int32))
    )
    used = (lax.dynamic_slice_in_dim(block_of, me_dp * slot_count, slot_count, axis=0) >= 0).astype(jnp.int32)
    here = jnp.stack([me_dp, me_pair]).astype(jnp.int32)
    if by_pieces:
        me = here
        columns = lax.dynamic_slice_in_dim(master, me_pair * 128, 128, axis=2).astype(BF)
        columns = columns.reshape(slot_count, 8, 16, 128).transpose(1, 0, 2, 3)
        slots = lax.all_to_all(columns, "dp", 0, 0).reshape(slots_all, 16, 128)
        early_index, late_index = split_order(slot_index)
        early_lists = gather_list(jnp.take(slots, early_index, axis=0))
        late_lists = gather_list(jnp.take(slots, late_index, axis=0))
    else:
        me = jnp.zeros_like(here)
        quarter = lax.dynamic_slice_in_dim(master, me_pair * 32, 32, axis=1).astype(BF)
        slots = lax.all_gather(quarter, "dp", axis=0, tiled=True)
        mine = jnp.take(slots, slot_index, axis=0)
        early, late = split_order(lax.all_gather(mine, "pair", axis=1, tiled=True))
        early_lists, late_lists = as_lists(early), as_lists(late)
    shared = lax.all_gather(observations, "pair", axis=2, tiled=True)

    x, cs, cd, lens, inv, cond, slope = prepare(actions, shared, tsteps, lengths, cot_skip, cot_down)
    width = samp
    normed, rstd, hid, mod, w_early = run_first(me, early_lists, x, cond, lens, inv, small_master, width)
    skip, dskip, g2, *late_grads, gs_late, w_late = run_second(
        me, late_lists, hid, x, cs, cd, lens, inv, small_master, width
    )
    g1, dmod, *early_grads, gs_early = run_third(
        me, w_late, g2, x, cond, normed, rstd, mod, lens, inv, small_master, width
    )
    down, dx, dobs = run_fourth(w_early, w_late, skip, g1, dskip, dmod, slope, lens, small_master, width)
    skip_out = skip.transpose(1, 0, 2).reshape(micro, samp, H, C)
    down_out = down.transpose(1, 0, 2).reshape(micro, samp, HD, C)
    actions_grad = dx.transpose(1, 0, 2).reshape(micro, samp, H, CI)
    g_small = jnp.concatenate([gs_early[0:5], gs_late[0:5]], axis=0)
    grad_small = sum_all(g_small)
    observations_grad = lax.psum_scatter(
        dobs.reshape(micro, samp, -1), "pair", scatter_dimension=2, tiled=True
    )

    if by_pieces:
        grads = join_order(reduce_list(early_grads), reduce_list(late_grads))
        spread = jnp.take(grads, jnp.maximum(block_of, 0), axis=0).reshape(dp_count, slot_count, 16, 128)
        owned = lax.all_to_all(spread, "dp", 0, 0)
        own = jnp.stack([owned, along_x(owned)])
        recv = core(own)
    else:
        grads = join_order(from_lists(early_grads), from_lists(late_grads))
        rows = grads.reshape(-1, 4, 32, C).transpose(1, 0, 2, 3)
        rows = lax.psum_scatter(rows, "pair", scatter_dimension=0)
        spread = jnp.take(rows, jnp.maximum(block_of, 0), axis=0)
        owned = lax.psum_scatter(spread, "dp", scatter_dimension=0, tiled=True)
        owned = lax.all_gather(owned, "pair", axis=1, tiled=True)
        cut = pieces_of(owned)
        own = jnp.stack([cut[:, 0], cut[:, 2]])
        recv = jnp.stack([cut[:, 1], cut[:, 3]])
    new_one, new_two, new_master = run_adamw(me, used, own, recv, master, moment_one, moment_two)
    small_first, small_second, new_small = adamw(
        small_master, small_one, small_two, grad_small, RATE_SMALL
    )
    return (
        skip_out,
        down_out,
        actions_grad,
        observations_grad,
        new_one,
        new_two,
        new_master,
        small_first,
        small_second,
        new_small,
    )


def solution(mesh):
    placed = (
        P(None, ("dp", "pair"), None, None),
        P(None, "dp", "pair"),
        P(None, ("dp", "pair")),
        P(None, ("dp", "pair")),
        P(None, ("dp", "pair"), None, None),
        P(None, ("dp", "pair"), None, None),
        P(),
        P("dp", None, None),
        P("dp", None, None),
        P("dp", None, None),
        P(),
        P(),
        P(),
    )
    return jax.shard_map(
        body,
        mesh=mesh,
        in_specs=placed,
        out_specs=(
            P(None, ("dp", "pair"), None, None),
            P(None, ("dp", "pair"), None, None),
            P(None, ("dp", "pair"), None, None),
            P(None, "dp", "pair"),
            P("dp", None, None),
            P("dp", None, None),
            P("dp", None, None),
            P(),
            P(),
            P(),
        ),
        check_vma=False,
    )
```

time: 510 us -> 341 us (0.67); the launches traced: 509 us -> 334 us
  waiting for transfers between devices: 285 us -> 82.6 us
  starting transfers between devices: 0.28 us -> 44 us
  blocking collectives: 49.4 us -> 23.9 us
  Pallas kernels: 102 us -> 121 us
  other arithmetic: 24.7 us -> 17.3 us
    reduce_scatter x4 -> x1, waiting for transfers between devices: 175 us -> 0.01 us  [body(): lax.psum_scatter(dobs.reshape(micro, samp, -1), 'pair', scatter_dimension...]
    all_gather x3 -> x0, waiting for transfers between devices: 110 us -> none  [the longest x1 75.8 us: body(): slots = lax.all_gather(quarter, 'dp', axis=0, tiled=True)]
    ppermute x0 -> x39, waiting for transfers between devices: none -> 77.1 us  [flip(): return lax.ppermute(value, axis, [(i, i ^ bit) for i in range(size)])]
    psum x1 -> x0, blocking collectives: 40.4 us -> none  [body(): grad_small = lax.psum(g_small, ('dp', 'pair'))]
    ppermute x0 -> x39, starting transfers between devices: none -> 36.7 us  [flip(): return lax.ppermute(value, axis, [(i, i ^ bit) for i in range(size)])]
    pallas_call x4 -> x5, Pallas kernels: 102 us -> 121 us  [call(): pl.pallas_call(kernel, grid_spec=pltpu.PrefetchScalarGridSpec(num_scalar_...]
    all_to_all x0 -> x1, blocking collectives: none -> 17.5 us  [body(): owned = lax.all_to_all(spread, 'dp', 0, 0)]
    sub x2 -> x1, other arithmetic: 10.6 us -> 0.66 us  [adamw(): return (first_new, second_new, weight - rate * update)]
  transfers between devices with their start and end apart: 7 -> 41, of which waited for: 5 -> 23; matrix products, arithmetic and copies ran while one was open for 8% -> 11% of each run, Pallas kernels for 3% -> 14%
where the time goes in v2:
time: 341 us; the launch traced here: 334 us
  Pallas kernels  121 us (35%)
  waiting for transfers between devices  82.6 us (24%)
  starting transfers between devices  44 us (13%)
  local copies, waits for them, and re-layouts  30 us (9%)
  blocking collectives  23.9 us (7%)
  other arithmetic  17.3 us (5%)
  between operations  15.2 us (4%)
    pallas_call x5, Pallas kernels, call(): pl.pallas_call(kernel, grid_spec=pltpu.PrefetchScalarGridSpec(num_scalar_...  121 us
    ppermute x39, waiting for transfers between devices, flip(): return lax.ppermute(value, axis, [(i, i ^ bit) for i in range(size)])  77.1 us
    ppermute x39, starting transfers between devices, flip(): return lax.ppermute(value, axis, [(i, i ^ bit) for i in range(size)])  36.7 us
    unnamed x62, local copies, waits for them, and re-layouts  22.2 us
    all_to_all x1, blocking collectives, body(): owned = lax.all_to_all(spread, 'dp', 0, 0)  17.5 us
    all_to_all x1, starting transfers between devices, body(): slots = lax.all_to_all(columns, 'dp', 0, 0).reshape(slots_all, 16, 128)  7.28 us
  transfers between devices with their start and end apart: 41, of which 23 were waited for; matrix products, arithmetic and copies ran while one was open for 11% of the time, Pallas kernels for 14%

profile of v2, /device:TPU:0, one launch (start us, length us, event | category | flops | bytes accessed | tf_op | source)
XLA Modules:
  0.0 334.3 jit_solution(3494600624054517034)
XLA Ops:
  9.4 7.3 %all-to-all-start = ((bf16[8,16,16,128]{3,2,1,0:T(8,128)(2,1)}), bf16[8,16,16,128]{3,2,1,0:T(8,128)(2,1)S(1)}, u32[]{:S(2)}, u32[]{:S(2)}) async-start(bf16[8,16,16,128]{3,2,1,0:T(8,128)(2,1)} %copy.49), calls=%async_computation | async-start | bytes 1048576 | tf_op jit(solution)/shard_map/all_to_all | solution.py:731
  17.4 6.5 %all_gather.3 = bf16[4,48,1024]{2,1,0:T(8,128)(2,1)S(1)} all-gather(bf16[4,48,256]{2,1,0:T(8,128)(2,1)S(1)} %copy-done.15), channel_id=1, replica_groups=mesh['dp'=8,'pair'=4] {'pair'}, dimensions={2}, use_global_device_ids=true | all-gather | bytes 491520 | tf_op jit(solution)/shard_map/all_gather | solution.py:742
  23.8 1.8 fusion.6
  25.7 5.5 %all-to-all-done = bf16[8,16,16,128]{3,2,1,0:T(8,128)(2,1)S(1)} async-done(((bf16[8,16,16,128]{3,2,1,0:T(8,128)(2,1)}), bf16[8,16,16,128]{3,2,1,0:T(8,128)(2,1)S(1)}, u32[]{:S(2)}, u32[]{:S(2)}) %all-to-all-start) | async-done | bytes 524320 | tf_op jit(solution)/shard_map/all_to_all | solution.py:731
  32.8 2.8 collective-permute-start
  35.6 7.4 %collective-permute-done.8 = bf16[1,28,16,128]{3,2,1,0:T(8,128)(2,1)S(1)} collective-permute-done((bf16[1,28,16,128]{3,2,1,0:T(8,128)(2,1)S(1)}, bf16[1,28,16,128]{3,2,1,0:T(8,128)(2,1)S(1)}, u32[]{:S(2)}, u32[]{:S(2)}) %collective-permute-start.8) | collective-permute-done | bytes 114720 | tf_op jit(solution)/shard_map/ppermute | solution.py:605
  45.8 5.4 %collective-permute-done.9 = bf16[2,28,16,128]{3,2,1,0:T(8,128)(2,1)S(1)} collective-permute-done((bf16[2,28,16,128]{3,2,1,0:T(8,128)(2,1)S(1)}, bf16[2,28,16,128]{3,2,1,0:T(8,128)(2,1)S(1)}, u32[]{:S(2)}, u32[]{:S(2)}) %collective-permute-start.9) | collective-permute-done | bytes 229408 | tf_op jit(solution)/shard_map/ppermute | solution.py:605
  55.9 3.3 collective-permute-start.2
  61.0 4.5 %collective-permute-done.5 = bf16[4,17,16,128]{3,2,1,0:T(8,128)(2,1)S(1)} collective-permute-done((bf16[4,17,16,128]{3,2,1,0:T(8,128)(2,1)S(1)}, bf16[4,17,16,128]{3,2,1,0:T(8,128)(2,1)S(1)}, u32[]{:S(2)}, u32[]{:S(2)}) %collective-permute-start.5) | collective-permute-done | bytes 278560 | tf_op jit(solution)/shard_map/ppermute | solution.py:605
  65.5 1.9 collective-permute-start.6
  71.5 3.4 %copy.51 = bf16[4,48,16,512]{3,1,0,2:T(8,128)(2,1)} copy(bf16[4,48,16,512]{3,2,1,0:T(8,128)(2,1)S(1)} %copy-done.1) | data formatting | bytes 6291456 | tf_op args[4]
  77.7 9.2 %collective-permute-done.6 = bf16[8,17,16,128]{3,2,1,0:T(8,128)(2,1)S(1)} collective-permute-done((bf16[8,17,16,128]{3,2,1,0:T(8,128)(2,1)S(1)}, bf16[8,17,16,128]{3,2,1,0:T(8,128)(2,1)S(1)}, u32[]{:S(2)}, u32[]{:S(2)}) %collective-permute-start.6) | collective-permute-done | bytes 557088 | tf_op jit(solution)/shard_map/ppermute | solution.py:605
  92.3 16.7 %first.1 = (f32[16,192,512]{2,1,0:T(8,128)}, f32[192,512]{1,0:T(8,128)}, bf16[16,192,512]{2,1,0:T(8,128)(2,1)}, f32[2,192,512]{2,1,0:T(8,128)}, bf16[28,8,16,512]{3,2,1,0:T(8,128)(2,1)}) custom-call(s32[2]{0:T(128)} %pad_add_fusion.me, bf16[16,14,16,128]{3,2,1,0:T(8,128)(2,1)} %copy-done.12, bf16[16,14,16,128]{3,2,1,0:T(8,128)(2,1)} %copy-done.27, ...), custom_call_target="tpu_custom_call" | custom-call | flops 4026531840 | bytes 20971520 | tf_op jit(solution)/shard_map/first/pallas_call | solution.py:488
  110.4 44.4 %second.1 = (bf16[16,192,512]{2,1,0:T(8,128)(2,1)}, bf16[16,192,512]{2,1,0:T(8,128)(2,1)}, bf16[16,192,512]{2,1,0:T(8,128)(2,1)}, bf16[16,17,16,128]{3,2,1,0:T(8...) custom-call(s32[2]{0:T(128)} %pad_add_fusion.me, ...), custom_call_target="tpu_custom_call" | custom-call | flops 24159191040 | bytes 20971520 | tf_op jit(solution)/shard_map/second/pallas_call | solution.py:488
  154.8 31.2 %third.1 = (bf16[16,192,512]{2,1,0:T(8,128)(2,1)}, bf16[2,192,512]{2,1,0:T(8,128)(2,1)}, bf16[16,14,16,128]{3,2,1,0:T(8,128)(2,1)}, bf16[16,14,16,128]{3,2,1,0:T...) custom-call(s32[2]{0:T(128)} %pad_add_fusion.me, ...), custom_call_target="tpu_custom_call" | custom-call | flops 16106127360 | bytes 20971520 | tf_op jit(solution)/shard_map/third/pallas_call | solution.py:488
  201.3 2.6 collective-permute-done.17
  210.6 13.8 %collective-permute-done.18 = bf16[4,14,16,128]{3,2,1,0:T(8,128)(2,1)S(1)} collective-permute-done((bf16[4,14,16,128]{3,2,1,0:T(8,128)(2,1)S(1)}, bf16[4,14,16,128]{3,2,1,0:T(8,128)(2,1)S(1)}, u32[]{:S(2)}, u32[]{:S(2)}) %collective-permute-start.18) | collective-permute-done | bytes 229408 | tf_op jit(solution)/shard_map/ppermute | solution.py:605
  227.4 4.0 %collective-permute-done.22 = bf16[2,28,16,128]{3,2,1,0:T(8,128)(2,1)S(1)} collective-permute-done((bf16[2,28,16,128]{3,2,1,0:T(8,128)(2,1)S(1)}, bf16[2,28,16,128]{3,2,1,0:T(8,128)(2,1)S(1)}, u32[]{:S(2)}, u32[]{:S(2)}) %collective-permute-start.22) | collective-permute-done | bytes 229408 | tf_op jit(solution)/shard_map/ppermute | solution.py:605
  236.1 2.2 collective-permute-done.23
  238.3 4.7 %collective-permute-done.30 = bf16[2,34,16,128]{3,2,1,0:T(8,128)(2,1)S(1)} collective-permute-done((bf16[2,34,16,128]{3,2,1,0:T(8,128)(2,1)S(1)}, bf16[2,34,16,128]{3,2,1,0:T(8,128)(2,1)S(1)}, u32[]{:S(2)}, u32[]{:S(2)}) %collective-permute-start.30) | collective-permute-done | bytes 278560 | tf_op jit(solution)/shard_map/ppermute | solution.py:605
  243.4 7.2 %collective-permute-done.31 = bf16[1,34,16,128]{3,2,1,0:T(8,128)(2,1)S(1)} collective-permute-done((bf16[1,34,16,128]{3,2,1,0:T(8,128)(2,1)S(1)}, bf16[1,34,16,128]{3,2,1,0:T(8,128)(2,1)S(1)}, u32[]{:S(2)}, u32[]{:S(2)}) %collective-permute-start.31) | collective-permute-done | bytes 139296 | tf_op jit(solution)/shard_map/ppermute | solution.py:605
  251.5 17.5 %all_to_all.10 = bf16[8,16,16,128]{3,2,1,0:T(8,128)(2,1)S(1)} all-to-all(bf16[8,16,16,128]{3,2,1,0:T(8,128)(2,1)S(1)} %broadcast_select_fusion), channel_id=1, replica_groups=mesh['dp'=8,'pair'=4] {'dp'}, dimensions={0} | all-to-all | bytes 1048576 | tf_op jit(solution)/shard_map/all_to_all | solution.py:766
  269.0 14.7 %fourth.1 = (bf16[8,192,512]{2,1,0:T(8,128)(2,1)}, f32[16,192,256]{2,1,0:T(8,128)}, f32[192,1024]{1,0:T(8,128)}) custom-call(bf16[28,8,16,512]{3,2,1,0:T(8,128)(2,1)} %get-tuple-element.39.w_early, bf16[34,8,16,512]{3,2,1,0:T(8,128)(2,1)} %get-tuple-element.40.w_hbm.w_late, bf16[16,192,512]{2,1,0:T(8,128)(2,1)} %get-tuple-element.38.skip_ref, ...), custom_call_target="tpu_custom_call" | custom-call | flops 8053063680 | bytes 20971520 | tf_op jit(solution)/shard_map/fourth/pallas_call | solution.py:488
  284.5 2.1 collective-permute-done.34
  286.6 2.1 collective-permute-start.35
  288.7 1.9 collective-permute-done.35
  292.1 2.4 collective-permute-done.36
  295.7 2.8 collective-permute-done.37
  300.2 5.5 %copy.55 = f32[4,48,16,256]{3,2,1,0:T(8,128)} copy(f32[4,48,16,256]{3,1,0,2:T(8,128)} %bitcast.53) | data formatting | bytes 6291456
  305.7 2.0 copy.54
  307.8 3.4 %copy.53 = bf16[4,48,16,512]{3,2,1,0:T(8,128)(2,1)} copy(bf16[4,48,16,512]{3,1,0,2:T(8,128)(2,1)S(1)} %bitcast.51) | data formatting | bytes 6291456
  312.9 14.1 %adamw.1 = (f32[16,128,512]{2,1,0:T(8,128)}, f32[16,128,512]{2,1,0:T(8,128)}, f32[16,128,512]{2,1,0:T(8,128)}) custom-call(s32[2]{0:T(128)} %pad_add_fusion.me, s32[16]{0:T(128)} %compare_convert_fusion.used, bf16[2,8,16,16,128]{4,3,2,1,0:T(8,128)(2,1)} %copy-done, bf16[2,8,16,16,128]{4,3,2,1,0:T(8,128)(2,1)} %copy-done.10, f32[16,128,512]{2,1,0:T(8,128)} %master_ref.1, ...), custom_call_target="tpu_custom_call" | custom-call | flops 20971520 | bytes 20971520 | tf_op jit(solution)/shard_map/adamw/pallas_call | solution.py:488
  (211 shorter events, 64.7 us)
Async XLA Ops:
  9.4 21.8 %all-to-all-start = ((bf16[8,16,16,128]{3,2,1,0:T(8,128)(2,1)}), bf16[8,16,16,128]{3,2,1,0:T(8,128)(2,1)S(1)}, u32[]{:S(2)}, u32[]{:S(2)}) async-start(bf16[8,16,16,128]{3,2,1,0:T(8,128)(2,1)} %copy.49), calls=%async_computation | async-start | bytes 1048576 | tf_op jit(solution)/shard_map/all_to_all | solution.py:731
  16.7 310.3 %reduce-scatter.2.cloned.1.call-start = ((), (), s32[]{:S(2)}) async-start(), calls=%async_computation.3 | async-start | bytes 983040 | tf_op jit(solution)/shard_map/reduce_scatter | solution.py:759
  31.9 11.2 %collective-permute-start.8 = (bf16[1,28,16,128]{3,2,1,0:T(8,128)(2,1)S(1)}, bf16[1,28,16,128]{3,2,1,0:T(8,128)(2,1)S(1)}, u32[]{:S(2)}, u32[]{:S(2)}) collective-permute-start(bf16[1,28,16,128]{3,2,1,0:T(8,128)(2,1)S(1)} %bitcast_select_fusion.2), channel_id=1, source_target_pairs={{0,16},{4,20},{8,24},{12,28},{16,0},{20,4},{24,8},{28,12},{1,17},{... | collective-permute-start | bytes 344072 | tf_op jit(solution)/shard_map/ppermute | solution.py:605
  32.8 11.7 %collective-permute-start = (bf16[1,34,16,128]{3,2,1,0:T(8,128)(2,1)S(1)}, bf16[1,34,16,128]{3,2,1,0:T(8,128)(2,1)S(1)}, u32[]{:S(2)}, u32[]{:S(2)}) collective-permute-start(bf16[1,34,16,128]{3,2,1,0:T(8,128)(2,1)S(1)} %bitcast_select_fusion.1), channel_id=1, source_target_pairs={{0,16},{4,20},{8,24},{12,28},{16,0},{20,4},{24,8},{28,12},{1,17},{... | collective-permute-start | bytes 417800 | tf_op jit(solution)/shard_map/ppermute | solution.py:605
  43.0 8.2 %collective-permute-start.9 = (bf16[2,28,16,128]{3,2,1,0:T(8,128)(2,1)S(1)}, bf16[2,28,16,128]{3,2,1,0:T(8,128)(2,1)S(1)}, u32[]{:S(2)}, u32[]{:S(2)}) collective-permute-start(bf16[2,28,16,128]{3,2,1,0:T(8,128)(2,1)S(1)} %pad_maximum_fusion.16), channel_id=1, source_target_pairs={{0,8},{4,12},{8,0},{12,4},{16,24},{20,28},{24,16},{28,20},{1,9},{5... | collective-permute-start | bytes 688136 | tf_op jit(solution)/shard_map/ppermute | solution.py:605
  44.5 9.6 %collective-permute-start.1 = (bf16[2,34,16,128]{3,2,1,0:T(8,128)(2,1)S(1)}, bf16[2,34,16,128]{3,2,1,0:T(8,128)(2,1)S(1)}, u32[]{:S(2)}, u32[]{:S(2)}) collective-permute-start(bf16[2,34,16,128]{3,2,1,0:T(8,128)(2,1)S(1)} %pad_maximum_fusion.13), channel_id=1, source_target_pairs={{0,8},{4,12},{8,0},{12,4},{16,24},{20,28},{24,16},{28,20},{1,9},{5... | collective-permute-start | bytes 835592 | tf_op jit(solution)/shard_map/ppermute | solution.py:605
  51.3 8.5 %collective-permute-start.13 = (bf16[4,14,16,128]{3,2,1,0:T(8,128)(2,1)S(1)}, bf16[4,14,16,128]{3,2,1,0:T(8,128)(2,1)S(1)}, u32[]{:S(2)}, u32[]{:S(2)}) collective-permute-start(bf16[4,14,16,128]{3,2,1,0:T(8,128)(2,1)S(1)} %get-tuple-element.123), channel_id=1, source_target_pairs={{0,2},{1,3},{2,0},{3,1},{4,6},{5,7},{6,4},{7,5},{8,10},{9,11},{10,... | collective-permute-start | bytes 688136 | tf_op jit(solution)/shard_map/ppermute | solution.py:605
  54.3 11.1 %collective-permute-start.5 = (bf16[4,17,16,128]{3,2,1,0:T(8,128)(2,1)S(1)}, bf16[4,17,16,128]{3,2,1,0:T(8,128)(2,1)S(1)}, u32[]{:S(2)}, u32[]{:S(2)}) collective-permute-start(bf16[4,17,16,128]{3,2,1,0:T(8,128)(2,1)S(1)} %get-tuple-element.121), channel_id=1, source_target_pairs={{0,2},{1,3},{2,0},{3,1},{4,6},{5,7},{6,4},{7,5},{8,10},{9,11},{10,... | collective-permute-start | bytes 835592 | tf_op jit(solution)/shard_map/ppermute | solution.py:605
  55.9 11.5 %collective-permute-start.2 = (bf16[4,17,16,128]{3,2,1,0:T(8,128)(2,1)S(1)}, bf16[4,17,16,128]{3,2,1,0:T(8,128)(2,1)S(1)}, u32[]{:S(2)}, u32[]{:S(2)}) collective-permute-start(bf16[4,17,16,128]{3,2,1,0:T(8,128)(2,1)S(1)} %get-tuple-element.122), channel_id=1, source_target_pairs={{0,4},{4,0},{8,12},{12,8},{16,20},{20,16},{24,28},{28,24},{1,5},{5... | collective-permute-start | bytes 835592 | tf_op jit(solution)/shard_map/ppermute | solution.py:605
  59.9 16.9 %collective-permute-start.14 = (bf16[8,14,16,128]{3,2,1,0:T(8,128)(2,1)S(1)}, bf16[8,14,16,128]{3,2,1,0:T(8,128)(2,1)S(1)}, u32[]{:S(2)}, u32[]{:S(2)}) collective-permute-start(bf16[8,14,16,128]{3,2,1,0:T(8,128)(2,1)S(1)} %pad_maximum_fusion.10), channel_id=1, source_target_pairs={{0,4},{4,0},{8,12},{12,8},{16,20},{20,16},{24,28},{28,24},{1,5},{5... | collective-permute-start | bytes 1376264 | tf_op jit(solution)/shard_map/ppermute | solution.py:605
  60.0 17.0 %collective-permute-start.11 = (bf16[8,14,16,128]{3,2,1,0:T(8,128)(2,1)S(1)}, bf16[8,14,16,128]{3,2,1,0:T(8,128)(2,1)S(1)}, u32[]{:S(2)}, u32[]{:S(2)}) collective-permute-start(bf16[8,14,16,128]{3,2,1,0:T(8,128)(2,1)S(1)} %pad_maximum_fusion.9), channel_id=1, source_target_pairs={{0,2},{1,3},{2,0},{3,1},{4,6},{5,7},{6,4},{7,5},{8,10},{9,11},{10,... | collective-permute-start | bytes 1376264 | tf_op jit(solution)/shard_map/ppermute | solution.py:605
  65.5 21.3 %collective-permute-start.6 = (bf16[8,17,16,128]{3,2,1,0:T(8,128)(2,1)S(1)}, bf16[8,17,16,128]{3,2,1,0:T(8,128)(2,1)S(1)}, u32[]{:S(2)}, u32[]{:S(2)}) collective-permute-start(bf16[8,17,16,128]{3,2,1,0:T(8,128)(2,1)S(1)} %pad_maximum_fusion.7), channel_id=1, source_target_pairs={{0,4},{4,0},{8,12},{12,8},{16,20},{20,16},{24,28},{28,24},{1,5},{5... | collective-permute-start | bytes 1671176 | tf_op jit(solution)/shard_map/ppermute | solution.py:605
  67.4 19.6 %collective-permute-start.3 = (bf16[8,17,16,128]{3,2,1,0:T(8,128)(2,1)S(1)}, bf16[8,17,16,128]{3,2,1,0:T(8,128)(2,1)S(1)}, u32[]{:S(2)}, u32[]{:S(2)}) collective-permute-start(bf16[8,17,16,128]{3,2,1,0:T(8,128)(2,1)S(1)} %pad_maximum_fusion.6), channel_id=1, source_target_pairs={{0,2},{1,3},{2,0},{3,1},{4,6},{5,7},{6,4},{7,5},{8,10},{9,11},{10,... | collective-permute-start | bytes 1671176 | tf_op jit(solution)/shard_map/ppermute | solution.py:605
  76.9 13.4 %collective-permute-start.15 = (bf16[16,14,16,128]{3,2,1,0:T(8,128)(2,1)S(1)}, bf16[16,14,16,128]{3,2,1,0:T(8,128)(2,1)S(1)}, u32[]{:S(2)}, u32[]{:S(2)}) collective-permute-start(bf16[16,14,16,128]{3,2,1,0:T(8,128)(2,1)S(1)} %pad_maximum_fusion.4.pc), channel_id=1, source_target_pairs={{0,1},{1,0},{2,3},{3,2},{4,5},{5,4},{6,7},{7,6},{8,9},{9,8},{10,11... | collective-permute-start | bytes 2752520 | tf_op jit(solution)/shard_map/ppermute | solution.py:605
  77.1 13.2 %collective-permute-start.12 = (bf16[16,14,16,128]{3,2,1,0:T(8,128)(2,1)S(1)}, bf16[16,14,16,128]{3,2,1,0:T(8,128)(2,1)S(1)}, u32[]{:S(2)}, u32[]{:S(2)}) collective-permute-start(bf16[16,14,16,128]{3,2,1,0:T(8,128)(2,1)S(1)} %pad_maximum_fusion.3.pa), channel_id=1, source_target_pairs={{0,1},{1,0},{2,3},{3,2},{4,5},{5,4},{6,7},{7,6},{8,9},{9,8},{10,11... | collective-permute-start | bytes 2752520 | tf_op jit(solution)/shard_map/ppermute | solution.py:605
  86.9 22.1 %collective-permute-start.7 = (bf16[16,17,16,128]{3,2,1,0:T(8,128)(2,1)S(1)}, bf16[16,17,16,128]{3,2,1,0:T(8,128)(2,1)S(1)}, u32[]{:S(2)}, u32[]{:S(2)}) collective-permute-start(bf16[16,17,16,128]{3,2,1,0:T(8,128)(2,1)S(1)} %pad_maximum_fusion.1.pc), channel_id=1, source_target_pairs={{0,1},{1,0},{2,3},{3,2},{4,5},{5,4},{6,7},{7,6},{8,9},{9,8},{10,11... | collective-permute-start | bytes 3342344 | tf_op jit(solution)/shard_map/ppermute | solution.py:605
  87.2 21.9 %collective-permute-start.4 = (bf16[16,17,16,128]{3,2,1,0:T(8,128)(2,1)S(1)}, bf16[16,17,16,128]{3,2,1,0:T(8,128)(2,1)S(1)}, u32[]{:S(2)}, u32[]{:S(2)}) collective-permute-start(bf16[16,17,16,128]{3,2,1,0:T(8,128)(2,1)S(1)} %pad_maximum_fusion.pa), channel_id=1, source_target_pairs={{0,1},{1,0},{2,3},{3,2},{4,5},{5,4},{6,7},{7,6},{8,9},{9,8},{10,11... | collective-permute-start | bytes 3342344 | tf_op jit(solution)/shard_map/ppermute | solution.py:605
  186.7 9.9 %collective-permute-start.24 = (bf16[16,17,16,128]{3,2,1,0:T(8,128)(2,1)}, bf16[16,17,16,128]{3,2,1,0:T(8,128)(2,1)}, u32[]{:S(2)}, u32[]{:S(2)}) collective-permute-start(bf16[16,17,16,128]{3,2,1,0:T(8,128)(2,1)} %get-tuple-element.56), channel_id=1, source_target_pairs={{0,1},{1,0},{2,3},{3,2},{4,5},{5,4},{6,7},{7,6},{8,9},{9,8},{10,11... | collective-permute-start | bytes 3342344 | tf_op jit(solution)/shard_map/ppermute | solution.py:605
  186.8 12.6 %collective-permute-start.27 = (bf16[16,17,16,128]{3,2,1,0:T(8,128)(2,1)}, bf16[16,17,16,128]{3,2,1,0:T(8,128)(2,1)}, u32[]{:S(2)}, u32[]{:S(2)}) collective-permute-start(bf16[16,17,16,128]{3,2,1,0:T(8,128)(2,1)} %get-tuple-element.58), channel_id=1, source_target_pairs={{0,1},{1,0},{2,3},{3,2},{4,5},{5,4},{6,7},{7,6},{8,9},{9,8},{10,11... | collective-permute-start | bytes 3342344 | tf_op jit(solution)/shard_map/ppermute | solution.py:605
  190.4 13.5 %collective-permute-start.17 = (bf16[8,14,16,128]{3,2,1,0:T(8,128)(2,1)S(1)}, bf16[8,14,16,128]{3,2,1,0:T(8,128)(2,1)}, u32[]{:S(2)}, u32[]{:S(2)}) collective-permute-start(bf16[8,14,16,128]{3,2,1,0:T(8,128)(2,1)S(1)} %slice.159), channel_id=1, source_target_pairs={{0,2},{1,3},{2,0},{3,1},{4,6},{5,7},{6,4},{7,5},{8,10},{9,11},{10,... | collective-permute-start | bytes 1376264 | tf_op jit(solution)/shard_map/ppermute | solution.py:605
  194.7 13.7 %collective-permute-start.20 = (bf16[8,14,16,128]{3,2,1,0:T(8,128)(2,1)}, bf16[8,14,16,128]{3,2,1,0:T(8,128)(2,1)}, u32[]{:S(2)}, u32[]{:S(2)}) collective-permute-start(bf16[8,14,16,128]{3,2,1,0:T(8,128)(2,1)} %slice.163), channel_id=1, source_target_pairs={{0,4},{4,0},{8,12},{12,8},{16,20},{20,16},{24,28},{28,24},{1,5},{5... | collective-permute-start | bytes 1376264 | tf_op jit(solution)/shard_map/ppermute | solution.py:605
  198.3 26.3 %collective-permute-start.25 = (bf16[8,17,16,128]{3,2,1,0:T(8,128)(2,1)S(1)}, bf16[8,17,16,128]{3,2,1,0:T(8,128)(2,1)S(1)}, u32[]{:S(2)}, u32[]{:S(2)}) collective-permute-start(bf16[8,17,16,128]{3,2,1,0:T(8,128)(2,1)S(1)} %slice.172), channel_id=1, source_target_pairs={{0,2},{1,3},{2,0},{3,1},{4,6},{5,7},{6,4},{7,5},{8,10},{9,11},{10,... | collective-permute-start | bytes 1671176 | tf_op jit(solution)/shard_map/ppermute | solution.py:605
  201.0 25.5 %collective-permute-start.28 = (bf16[8,17,16,128]{3,2,1,0:T(8,128)(2,1)S(1)}, bf16[8,17,16,128]{3,2,1,0:T(8,128)(2,1)S(1)}, u32[]{:S(2)}, u32[]{:S(2)}) collective-permute-start(bf16[8,17,16,128]{3,2,1,0:T(8,128)(2,1)S(1)} %slice.176), channel_id=1, source_target_pairs={{0,4},{4,0},{8,12},{12,8},{16,20},{20,16},{24,28},{28,24},{1,5},{5... | collective-permute-start | bytes 1671176 | tf_op jit(solution)/shard_map/ppermute | solution.py:605
  205.0 19.4 %collective-permute-start.18 = (bf16[4,14,16,128]{3,2,1,0:T(8,128)(2,1)S(1)}, bf16[4,14,16,128]{3,2,1,0:T(8,128)(2,1)S(1)}, u32[]{:S(2)}, u32[]{:S(2)}) collective-permute-start(bf16[4,14,16,128]{3,2,1,0:T(8,128)(2,1)S(1)} %slice.161), channel_id=1, source_target_pairs={{0,4},{4,0},{8,12},{12,8},{16,20},{20,16},{24,28},{28,24},{1,5},{5... | collective-permute-start | bytes 688136 | tf_op jit(solution)/shard_map/ppermute | solution.py:605
  209.5 14.9 %collective-permute-start.21 = (bf16[4,14,16,128]{3,2,1,0:T(8,128)(2,1)S(1)}, bf16[4,14,16,128]{3,2,1,0:T(8,128)(2,1)S(1)}, u32[]{:S(2)}, u32[]{:S(2)}) collective-permute-start(bf16[4,14,16,128]{3,2,1,0:T(8,128)(2,1)S(1)} %slice.165), channel_id=1, source_target_pairs={{0,2},{1,3},{2,0},{3,1},{4,6},{5,7},{6,4},{7,5},{8,10},{9,11},{10,... | collective-permute-start | bytes 688136 | tf_op jit(solution)/shard_map/ppermute | solution.py:605
  224.7 7.9 %collective-permute-start.26 = (bf16[4,17,16,128]{3,2,1,0:T(8,128)(2,1)S(1)}, bf16[4,17,16,128]{3,2,1,0:T(8,128)(2,1)S(1)}, u32[]{:S(2)}, u32[]{:S(2)}) collective-permute-start(bf16[4,17,16,128]{3,2,1,0:T(8,128)(2,1)S(1)} %slice.174), channel_id=1, source_target_pairs={{0,4},{4,0},{8,12},{12,8},{16,20},{20,16},{24,28},{28,24},{1,5},{5... | collective-permute-start | bytes 835592 | tf_op jit(solution)/shard_map/ppermute | solution.py:605
  226.6 7.6 %collective-permute-start.29 = (bf16[4,17,16,128]{3,2,1,0:T(8,128)(2,1)S(1)}, bf16[4,17,16,128]{3,2,1,0:T(8,128)(2,1)S(1)}, u32[]{:S(2)}, u32[]{:S(2)}) collective-permute-start(bf16[4,17,16,128]{3,2,1,0:T(8,128)(2,1)S(1)} %slice.178), channel_id=1, source_target_pairs={{0,2},{1,3},{2,0},{3,1},{4,6},{5,7},{6,4},{7,5},{8,10},{9,11},{10,... | collective-permute-start | bytes 835592 | tf_op jit(solution)/shard_map/ppermute | solution.py:605
  234.3 8.7 %collective-permute-start.30 = (bf16[2,34,16,128]{3,2,1,0:T(8,128)(2,1)S(1)}, bf16[2,34,16,128]{3,2,1,0:T(8,128)(2,1)S(1)}, u32[]{:S(2)}, u32[]{:S(2)}) collective-permute-start(bf16[2,34,16,128]{3,2,1,0:T(8,128)(2,1)S(1)} %pad_maximum_fusion.12), channel_id=1, source_target_pairs={{0,8},{4,12},{8,0},{12,4},{16,24},{20,28},{24,16},{28,20},{1,9},{5... | collective-permute-start | bytes 835592 | tf_op jit(solution)/shard_map/ppermute | solution.py:605
  243.1 7.4 %collective-permute-start.31 = (bf16[1,34,16,128]{3,2,1,0:T(8,128)(2,1)S(1)}, bf16[1,34,16,128]{3,2,1,0:T(8,128)(2,1)S(1)}, u32[]{:S(2)}, u32[]{:S(2)}) collective-permute-start(bf16[1,34,16,128]{3,2,1,0:T(8,128)(2,1)S(1)} %slice.182), channel_id=1, source_target_pairs={{0,16},{4,20},{8,24},{12,28},{16,0},{20,4},{24,8},{28,12},{1,17},{... | collective-permute-start | bytes 417800 | tf_op jit(solution)/shard_map/ppermute | solution.py:605
  269.0 14.7 %collective-permute-start.32 = (bf16[8,16,16,128]{3,2,1,0:T(8,128)(2,1)S(1)}, bf16[8,16,16,128]{3,2,1,0:T(8,128)(2,1)S(1)}, u32[]{:S(2)}, u32[]{:S(2)}) collective-permute-start(bf16[8,16,16,128]{3,2,1,0:T(8,128)(2,1)S(1)} %all_to_all.10), channel_id=1, source_target_pairs={{0,2},{1,3},{2,0},{3,1},{4,6},{5,7},{6,4},{7,5},{8,10},{9,11},{10,... | collective-permute-start | bytes 1572872 | tf_op jit(solution)/shard_map/ppermute | solution.py:605
  283.9 28.0 %collective-permute-start.33 = (bf16[2,8,16,16,128]{4,3,2,1,0:T(8,128)(2,1)S(1)}, bf16[2,8,16,16,128]{4,3,2,1,0:T(8,128)(2,1)S(1)}, u32[]{:S(2)}, u32[]{:S(2)}) collective-permute-start(bf16[2,8,16,16,128]{4,3,2,1,0:T(8,128)(2,1)S(1)} %pad_maximum_fusion.2.own_ref), channel_id=1, source_target_pairs={{0,1},{1,0},{2,3},{3,2},{4,5},{5,4},{6,7},{7,6},{8,9},{9,8},{10,11... | collective-permute-start | bytes 3145736 | tf_op jit(solution)/shard_map/ppermute | solution.py:605
  298.5 12.7 %collective-permute-start.38 = (f32[10,512]{1,0:T(8,128)S(1)}, f32[10,512]{1,0:T(8,128)S(1)}, u32[]{:S(2)}, u32[]{:S(2)}) collective-permute-start(f32[10,512]{1,0:T(8,128)S(1)} %add.164), channel_id=1, source_target_pairs={{0,16},{4,20},{8,24},{12,28},{16,0},{20,4},{24,8},{28,12},{1,17},{... | collective-permute-start | bytes 61448 | tf_op jit(solution)/shard_map/ppermute | solution.py:605
  (37 other events, 192.0 us)
Sparse Core Ops, SparseCore 0:
  283.9 22.7 reduce-scatter.1
